TPU v7x, 128 devices: a whole 4x4x4 slice. The times are simulated.
128 devices in a mesh: grp: 16 (over z, x_hi, core), sp: 8 (over y, x_lo).
Axes of the slice: x: 4 (x_hi: 2, x_lo: 2; x = x_hi * 2 + x_lo), y: 4, z: 4, core: 2. Of those that a mesh axis runs over, the one named last changes fastest.
Arguments:
- image_tokens: bfloat16 [32, 8, 64, 3072], P('grp', 'sp'), may hold values from -6 to 6
- text_tokens: bfloat16 [256, 3072], replicated, may hold values from -6 to 6
- mod_shift: float32 [3072], replicated, may hold values from -3 to 3
- mod_scale: float32 [3072], replicated, may hold values from -0.5 to 0.5
- mod_gate: float32 [3072], replicated, may hold values from 0.5 to 1.5
- w_qkv: bfloat16 [3072, 3, 2048], P(None, None, 'sp'), may hold values from -0.109375 to 0.109375
- w_text_kv: bfloat16 [3072, 2, 2048], P(None, None, 'sp'), may hold values from -0.109375 to 0.109375
- q_gain: float32 [128], replicated, may hold values from 1.5 to 2.5
- k_gain: float32 [128], replicated, may hold values from 1.5 to 2.5
- text_gain: float32 [128], replicated, may hold values from 1.5 to 2.5
- w_out: bfloat16 [2048, 3072], P('sp'), may hold values from -0.125 to 0.125
- w_final: bfloat16 [3072, 64], replicated, may hold values from -0.109375 to 0.109375
- w_conv_in: bfloat16 [3, 3, 3, 16, 256], replicated, may hold values from -0.3125 to 0.3125
- w_conv_mid: bfloat16 [3, 3, 3, 256, 256], replicated, may hold values from -0.078125 to 0.078125
- clip_ids: int32 [32], replicated, may hold values from 0 to 7, never falling along the last dimension, each value on 1 to 8 neighbouring positions
Outputs:
- block_out: bfloat16 [32, 8, 64, 3072], P('grp', 'sp')
- decoded: bfloat16 [32, 16, 128, 256], P('grp', 'sp')
Inputs may be any that keep to these rules, and one draw needn't show every extreme that they name: `clip_ids`: clip numbers never fall along the frames, every number from 0 to 7 appears, and each clip spans 1 to 8 consecutive frames.
All inputs are finite; a program needn't handle non-finite values.
Results may differ from a plain program's by a relative error of at most 0.02.
Values may be sent and summed in bfloat16 or wider, within the bound.
A program may use at most 128 MiB of HBM per device.

v0:
```python
import math

import jax
import jax.numpy as jnp
from jax import lax
from jax.sharding import PartitionSpec as P

HD = 128


EPS = 1e-06


def passed_along(value, axis, steps):
    count = lax.axis_size(axis)
    first, last = (max(0, -steps), min(count, count - steps))
    return lax.ppermute(value, axis, [(source, source + steps) for source in range(first, last)])


def with_halo(x, sides, width):
    for axis, dim in sides:
        size, length = (lax.axis_size(axis), x.shape[dim])
        up = [(i, (i + 1) % size) for i in range(size - 1)]
        down = [(j, i) for i, j in up]
        last = lax.slice_in_dim(x, length - width, length, axis=dim)
        first = lax.slice_in_dim(x, 0, width, axis=dim)
        before = lax.ppermute(last, axis, up)
        after = lax.ppermute(first, axis, down)
        x = jnp.concatenate([before, x, after], axis=dim)
    return x


def layer_norm(values):
    middle = jnp.mean(values, axis=-1, keepdims=True)
    centered = values - middle
    spread = jnp.mean(centered * centered, axis=-1, keepdims=True)
    return centered * lax.rsqrt(spread + EPS)


def rms_scale(values, gain):
    return values * lax.rsqrt(jnp.mean(values * values, axis=-1, keepdims=True) + EPS) * gain


def causal_conv(window, lowest, out_frames, weight, starts):
    count_out = out_frames.shape[0]
    height = window.shape[1] - 2
    breadth = window.shape[2]
    depth = weight.shape[3]
    width_out = weight.shape[4]
    padded = jnp.pad(window, ((0, 0), (0, 0), (1, 1), (0, 0)))
    frame_starts = jnp.take(starts, jnp.clip(out_frames, 0, starts.shape[0] - 1), axis=0)
    total = jnp.zeros((count_out * height * breadth, width_out), jnp.float32)
    for shift_t in range(3):
        index = jnp.maximum(out_frames - shift_t, frame_starts) - lowest
        taken = jnp.take(padded, index, axis=0, mode="clip")
        for shift_r in range(3):
            for shift_c in range(3):
                patch_view = taken[:, shift_r : shift_r + height, shift_c : shift_c + breadth, :]
                total = total + jnp.dot(
                    patch_view.reshape(-1, depth),
                    weight[shift_t, shift_r, shift_c],
                    preferred_element_type=jnp.float32,
                )
    return total.reshape(count_out, height, breadth, width_out)


def per_device(
    image_tokens,
    text_tokens,
    mod_shift,
    mod_scale,
    mod_gate,
    w_qkv,
    w_text_kv,
    q_gain,
    k_gain,
    text_gain,
    w_out,
    w_final,
    w_conv_in,
    w_conv_mid,
    clip_ids,
):
    slab, patch_rows, breadth, width = image_tokens.shape
    local = slab * patch_rows * breadth
    inner_here = w_qkv.shape[2]
    heads_here = inner_here // HD
    residual_in = image_tokens.reshape(local, width).astype(jnp.float32)
    normed = (layer_norm(residual_in) * (1.0 + mod_scale) + mod_shift).astype(jnp.bfloat16)
    qkv_weights = w_qkv.reshape(width, 3 * inner_here)
    projected = jnp.dot(
        lax.all_gather(normed, "sp", axis=0, tiled=True),
        qkv_weights,
        preferred_element_type=jnp.float32,
    )
    group_rows = projected.shape[0]
    projected = projected.reshape(group_rows, 3, heads_here, HD)
    queries = rms_scale(projected[:, 0], q_gain).astype(jnp.bfloat16)
    keys = rms_scale(projected[:, 1], k_gain).astype(jnp.bfloat16)
    values = projected[:, 2].astype(jnp.bfloat16)
    text_count = text_tokens.shape[0]
    text_normed = layer_norm(text_tokens.astype(jnp.float32)).astype(jnp.bfloat16)
    text_projected = jnp.dot(
        text_normed, w_text_kv.reshape(width, 2 * inner_here), preferred_element_type=jnp.float32
    ).reshape(text_count, 2, heads_here, HD)
    text_keys = rms_scale(text_projected[:, 0], text_gain).astype(jnp.bfloat16)
    text_values = text_projected[:, 1].astype(jnp.bfloat16)
    factor = HD ** (-0.5)

    def absorb(carry, key_rows, value_rows):
        count = key_rows.shape[0]
        block = math.gcd(count, 1024)
        key_blocks = key_rows.reshape(count // block, block, heads_here, HD)
        value_blocks = value_rows.reshape(count // block, block, heads_here, HD)

        def step(state, pair):
            weighted, totals = state
            key_block, value_block = pair
            scores = (
                jnp.einsum("qhd,khd->hqk", queries, key_block, preferred_element_type=jnp.float32)
                * factor
            )
            weights = jnp.exp(scores).astype(jnp.bfloat16)
            totals = totals + jnp.sum(weights.astype(jnp.float32), axis=-1)
            weighted = weighted + jnp.einsum(
                "hqk,khd->hqd", weights, value_block, preferred_element_type=jnp.float32
            )
            return ((weighted, totals), None)

        carry, unused = lax.scan(step, carry, (key_blocks, value_blocks))
        return carry

    start_state = (
        jnp.zeros((heads_here, group_rows, HD), jnp.float32),
        jnp.zeros((heads_here, group_rows), jnp.float32),
    )
    start_state = absorb(start_state, text_keys, text_values)
    weighted, totals = absorb(
        start_state,
        lax.all_gather(keys, "grp", axis=0, tiled=True),
        lax.all_gather(values, "grp", axis=0, tiled=True),
    )
    attended_heads = (weighted / totals[:, :, None]).astype(jnp.bfloat16)
    attended = jnp.transpose(attended_heads, (1, 0, 2)).reshape(group_rows, inner_here)
    proj = lax.psum_scatter(
        jnp.dot(attended, w_out, preferred_element_type=jnp.float32).astype(jnp.bfloat16),
        "sp",
        scatter_dimension=0,
        tiled=True,
    ).astype(jnp.float32)
    block_flat = (residual_in + mod_gate * proj).astype(jnp.bfloat16)
    final = layer_norm(block_flat.astype(jnp.float32)).astype(jnp.bfloat16)
    latent_flat = jnp.dot(final, w_final, preferred_element_type=jnp.float32).astype(jnp.bfloat16)
    latent_ch = w_final.shape[1] // 4
    latent = (
        latent_flat.reshape(slab, patch_rows, breadth, 2, 2, latent_ch)
        .transpose(0, 1, 3, 2, 4, 5)
        .reshape(slab, 2 * patch_rows, 2 * breadth, latent_ch)
    )
    starts = jnp.sum((clip_ids[None, :] < clip_ids[:, None]).astype(jnp.int32), axis=1)
    first_frame = lax.axis_index("grp") * slab
    own_frames = first_frame + jnp.arange(slab, dtype=jnp.int32)
    earlier = passed_along(latent, "grp", 1)
    framed = with_halo(jnp.concatenate([earlier, latent], axis=0), (("sp", 1),), 1)
    first_conv = causal_conv(framed, first_frame - slab, own_frames, w_conv_in, starts)
    activated = jax.nn.silu(first_conv).astype(jnp.bfloat16)
    earlier_act = passed_along(activated, "grp", 1)
    framed_act = with_halo(jnp.concatenate([earlier_act, activated], axis=0), (("sp", 1),), 1)
    second_conv = causal_conv(framed_act, first_frame - slab, own_frames, w_conv_mid, starts)
    decoded = (second_conv + first_conv).astype(jnp.bfloat16)
    block_out = block_flat.reshape(slab, patch_rows, breadth, width)
    return (block_out, decoded)


def solution(mesh):
    return jax.shard_map(
        per_device,
        mesh=mesh,
        in_specs=(
            P("grp", "sp", None, None),
            P(),
            P(),
            P(),
            P(),
            P(None, None, "sp"),
            P(None, None, "sp"),
            P(),
            P(),
            P(),
            P("sp", None),
            P(),
            P(),
            P(),
            P(),
        ),
        out_specs=(P("grp", "sp", None, None), P("grp", "sp", None, None)),
        check_vma=False,
    )
```

profile of v0, /device:TPU:41, one launch (start us, length us, event | category | flops | bytes accessed | tf_op | source)
XLA Modules:
  0.0 628.6 jit_solution(13650212823048352963)
XLA Ops:
  13.5 6.7 %copy.98 = bf16[3072,3,256]{0,2,1:T(8,128)(2,1)} copy(bf16[3072,3,256]{2,0,1:T(8,128)(2,1)} %param.24) | data formatting | bytes 9437184 | tf_op args[5]
  20.2 124.4 %all-gather.5.cloned.1.call-done = bf16[1024,3072]{1,0:T(8,128)(2,1)} async-done(((bf16[128,3072]{1,0:T(8,128)(2,1)}), bf16[1024,3072]{1,0:T(8,128)(2,1)}) %all-gather.5.cloned.1.call-update) | async-done | bytes 6291472 | tf_op jit(solution)/shard_map/all_gather | solution.py:92
  144.6 8.6 %fusion.6 = f32[1024,3,2,128]{0,3,2,1:T(8,128)S(1)} fusion(bf16[3,2,128,3072]{3,2,1,0:T(8,128)(2,1)} %bitcast.411, bf16[1024,3072]{1,0:T(8,128)(2,1)} %all-gather.5.cloned.1.call-done), kind=kOutput, calls=%fused_computation.16 | convolution fusion | flops 4831838208 | bytes 14155776 | tf_op jit(solution)/shard_map/dot_general | solution.py:91
  158.3 4.1 copy.146
  162.4 5.3 copy.99
  168.6 3.0 fusion.17
  176.9 52.4 %all-gather.7.cloned.1.call-done = bf16[16384,2,128]{0,2,1:T(8,128)(2,1)} async-done(((bf16[1024,2,128]{0,2,1:T(8,128)(2,1)}), bf16[16384,2,128]{0,2,1:T(8,128)(2,1)}) %all-gather.7.cloned.1.call-update) | async-done | bytes 8388624 | tf_op jit(solution)/shard_map/all_gather | solution.py:140
  229.3 15.2 %copy.147 = bf16[32,8,16,1024]{3,2,1,0:T(8,128)(2,1)} copy(bf16[32,8,16,1024]{3,1,2,0:T(8,128)(2,1)} %bitcast.409) | data formatting | bytes 16777216
  244.7 12.1 %copy.104 = bf16[16,1024,2,128]{3,1,2,0:T(8,128)(2,1)} copy(bf16[16,1024,2,128]{1,0,3,2:T(8,128)(2,1)} %bitcast.406) | data formatting | bytes 16777216 | tf_op jit(solution)/shard_map/while | solution.py:130
  256.8 45.9 %all-gather.9.cloned.1.call-done = bf16[16384,1,2,128]{0,3,2,1:T(8,128)(2,1)} async-done(((bf16[1024,1,2,128]{0,3,2,1:T(8,128)(2,1)}), bf16[16384,1,2,128]{0,3,2,1:T(8,128)(2,1)}) %all-gather.9.cloned.1.call-update) | async-done | bytes 8388624 | tf_op jit(solution)/shard_map/all_gather | solution.py:141
  302.7 15.2 %copy.148 = bf16[32,8,16,1024]{3,2,1,0:T(8,128)(2,1)} copy(bf16[32,8,16,1024]{3,1,2,0:T(8,128)(2,1)} %bitcast.410) | data formatting | bytes 16777216
  317.9 12.1 %copy.106 = bf16[16,1024,2,128]{3,1,2,0:T(8,128)(2,1)} copy(bf16[16,1024,2,128]{1,0,3,2:T(8,128)(2,1)} %bitcast.407) | data formatting | bytes 16777216 | tf_op jit(solution)/shard_map/while | solution.py:130
  330.0 88.8 %while.2 = (s32[]{:T(128)}, f32[2,1024,128]{2,1,0:T(8,128)S(1)}, f32[2,1024]{1,0:T(2,128)S(1)}, bf16[16,1024,2,128]{3,1,2,0:T(8,128)(2,1)}, bf16[1024,2,128]{2,0...) while((s32[]{:T(128)}, f32[2,1024,128]{2,1,0:T(8,128)S(1)}, f32[2,1024]{1,0:T(2,128)S(1)}, ...), condition=%wide.region_10.11_spmd, body=%wide.region_8.10_spmd.sunk | while | flops 1082392576 | bytes 12091485 | solution.py:130
  330.2 2.6 convert_reduce_fusion.7
  332.7 2.9 convolution_add_fusion.54
  338.3 2.9 convolution_add_fusion.54
  341.2 2.6 convert_reduce_fusion.7
  343.8 2.9 convolution_add_fusion.54
  346.8 2.6 convert_reduce_fusion.7
  349.4 2.9 convolution_add_fusion.54
  352.3 2.6 convert_reduce_fusion.7
  354.9 2.9 convolution_add_fusion.54
  357.9 2.6 convert_reduce_fusion.7
  360.4 2.9 convolution_add_fusion.54
  363.4 2.6 convert_reduce_fusion.7
  366.0 2.9 convolution_add_fusion.54
  368.9 2.6 convert_reduce_fusion.7
  371.5 2.9 convolution_add_fusion.54
  374.5 2.6 convert_reduce_fusion.7
  377.1 2.9 convolution_add_fusion.54
  382.6 2.9 convolution_add_fusion.54
  388.1 2.9 convolution_add_fusion.54
  393.7 2.9 convolution_add_fusion.54
  399.2 2.9 convolution_add_fusion.54
  404.8 2.9 convolution_add_fusion.54
  410.3 2.9 convolution_add_fusion.54
  415.8 2.9 convolution_add_fusion.54
  421.5 4.5 convolution_convert_fusion
  427.5 127.2 %reduce-scatter.2.cloned.1.call-done = bf16[128,3072]{1,0:T(8,128)(2,1)} async-done(((bf16[1024,3072]{1,0:T(8,128)(2,1)}), bf16[128,3072]{1,0:T(8,128)(2,1)}) %reduce-scatter.2.cloned.1.call-update) | async-done | bytes 786448 | tf_op jit(solution)/shard_map/reduce_scatter | solution.py:145
  557.8 4.8 collective-permute-start
  564.7 2.8 collective-permute-start.1
  567.5 3.4 collective-permute-start.2
  582.4 7.9 %collective-permute-start.3 = (bf16[2,2,128,256]{3,2,1,0:T(8,128)(2,1)S(1)}, bf16[2,2,128,256]{3,2,1,0:T(8,128)(2,1)S(1)}, u32[]{:S(2)}, u32[]{:S(2)}) collective-permute-start(bf16[2,2,128,256]{3,2,1,0:T(8,128)(2,1)S(1)} %multiply_convert_fusion.2), channel_id=1, source_target_pairs={{0,8},{8,16},{16,24},{24,32},{32,40},{40,48},{48,56},{56,64},{64,7... | collective-permute-start | bytes 786440 | tf_op jit(solution)/shard_map/ppermute | solution.py:17
  590.3 3.3 collective-permute-done.3
  593.7 3.1 collective-permute-start.4
  596.7 3.4 collective-permute-start.5
  601.7 4.7 collective-permute-done.5
  609.9 2.8 pad_slice_fusion.14
  (238 shorter events, 72.5 us)
Async XLA Ops:
  7.2 414.3 %copy-start = (bf16[256,3072]{1,0:T(8,128)(2,1)S(1)}, bf16[256,3072]{1,0:T(8,128)(2,1)}, u32[]{:S(2)}) copy-start(bf16[256,3072]{1,0:T(8,128)(2,1)} %param.29) | copy-start | bytes 4718596
  7.2 137.4 %all-gather.5.cloned.1.call-start = ((), (), s32[]{:S(2)}) async-start(), calls=%async_computation.1 | async-start | bytes 7077888 | tf_op jit(solution)/shard_map/all_gather | solution.py:92
  13.5 215.9 %all-gather.7.cloned.1.call-start = ((), (), s32[]{:S(2)}) async-start(), calls=%async_computation.2 | async-start | bytes 8912896 | tf_op jit(solution)/shard_map/all_gather | solution.py:140
  144.6 10.3 %copy-start.14 = (f32[128]{0:T(128)S(1)}, f32[128]{0:T(128)}, u32[]{:S(2)}) copy-start(f32[128]{0:T(128)} %param.27) | copy-start | bytes 1540
  144.6 10.3 %copy-start.15 = (f32[128]{0:T(128)S(1)}, f32[128]{0:T(128)}, u32[]{:S(2)}) copy-start(f32[128]{0:T(128)} %param.26) | copy-start | bytes 1540
  153.2 1.6 copy-start.2
  156.1 146.6 %all-gather.9.cloned.1.call-start = ((), (), s32[]{:S(2)}) async-start(), calls=%async_computation.4 | async-start | bytes 8912896 | tf_op jit(solution)/shard_map/all_gather | solution.py:141
  158.3 396.4 %reduce-scatter.2.cloned.1.call-start = ((), (), s32[]{:S(2)}) async-start(), calls=%async_computation.3 | async-start | bytes 7077888 | tf_op jit(solution)/shard_map/reduce_scatter | solution.py:145
  162.4 5.3 copy-start.4
  168.6 6.0 copy-start.17
  171.6 0.8 copy-start.9
  172.5 3.9 copy-start.10
  317.9 12.1 %copy-start.11 = (bf16[1024,2,128]{2,0,1:T(8,128)(2,1)S(1)}, bf16[1024,2,128]{2,0,1:T(8,128)(2,1)}, u32[]{:S(2)}) copy-start(bf16[1024,2,128]{2,0,1:T(8,128)(2,1)} %copy.105) | copy-start | bytes 1572868
  426.0 0.7 copy-start.18
  426.0 128.7 %copy-start.1 = (bf16[2,1,64,3072]{3,2,1,0:T(8,128)(2,1)S(1)}, bf16[2,1,64,3072]{3,2,1,0:T(8,128)(2,1)}, u32[]{:S(2)}) copy-start(bf16[2,1,64,3072]{3,2,1,0:T(8,128)(2,1)} %param.19) | copy-start | bytes 2359300
  426.0 128.7 %copy-start.13 = (f32[3072]{0:T(1024)S(1)}, f32[3072]{0:T(1024)}, u32[]{:S(2)}) copy-start(f32[3072]{0:T(1024)} %param.23) | copy-start | bytes 36868
  426.0 131.2 %copy-start.16 = (bf16[3072,64]{0,1:T(8,128)(2,1)S(1)}, bf16[3072,64]{0,1:T(8,128)(2,1)}, u32[]{:S(2)}) copy-start(bf16[3072,64]{0,1:T(8,128)(2,1)} %param.30) | copy-start | bytes 1179652
  556.2 0.9 copy-start.8
  556.3 18.9 %copy-start.12 = (bf16[3,3,3,16,256]{4,3,2,1,0:T(8,128)(2,1)S(1)}, bf16[3,3,3,16,256]{4,3,2,1,0:T(8,128)(2,1)}, u32[]{:S(2)}) copy-start(bf16[3,3,3,16,256]{4,3,2,1,0:T(8,128)(2,1)} %param.31) | copy-start | bytes 663556
  557.8 6.7 %collective-permute-start = (bf16[2,2,128,16]{3,2,1,0:T(8,128)(2,1)S(1)}, bf16[2,2,128,16]{3,2,1,0:T(8,128)(2,1)S(1)}, u32[]{:S(2)}, u32[]{:S(2)}) collective-permute-start(bf16[2,2,128,16]{3,2,1,0:T(8,128)(2,1)S(1)} %bitcast.446), channel_id=1, source_target_pairs={{0,8},{8,16},{16,24},{24,32},{32,40},{40,48},{48,56},{56,64},{64,7... | collective-permute-start | bytes 49160 | tf_op jit(solution)/shard_map/ppermute | solution.py:17
  564.7 6.2 collective-permute-start.1
  567.5 4.5 collective-permute-start.2
  582.3 19.4 %copy-start.5 = (f32[512,256]{1,0:T(8,128)}, f32[512,256]{1,0:T(8,128)S(1)}, u32[]{:S(2)}) copy-start(f32[512,256]{1,0:T(8,128)S(1)} %convolution_add_fusion.1) | copy-start | bytes 1572868
  582.4 11.2 %collective-permute-start.3 = (bf16[2,2,128,256]{3,2,1,0:T(8,128)(2,1)S(1)}, bf16[2,2,128,256]{3,2,1,0:T(8,128)(2,1)S(1)}, u32[]{:S(2)}, u32[]{:S(2)}) collective-permute-start(bf16[2,2,128,256]{3,2,1,0:T(8,128)(2,1)S(1)} %multiply_convert_fusion.2), channel_id=1, source_target_pairs={{0,8},{8,16},{16,24},{24,32},{32,40},{40,48},{48,56},{56,64},{64,7... | collective-permute-start | bytes 786440 | tf_op jit(solution)/shard_map/ppermute | solution.py:17
  593.7 8.0 %collective-permute-start.4 = (bf16[4,1,128,256]{3,2,1,0:T(8,128)(2,1)S(1)}, bf16[4,1,128,256]{3,2,1,0:T(8,128)(2,1)S(1)}, u32[]{:S(2)}, u32[]{:S(2)}) collective-permute-start(bf16[4,1,128,256]{3,2,1,0:T(8,128)(2,1)S(1)} %get-tuple-element.143), channel_id=1, source_target_pairs={{0,1},{1,2},{2,3},{3,4},{4,5},{5,6},{6,7},{8,9},{9,10},{10,11},{11... | collective-permute-start | bytes 786440 | tf_op jit(solution)/shard_map/ppermute | solution.py:27
  596.7 9.6 %collective-permute-start.5 = (bf16[4,1,128,256]{3,2,1,0:T(8,128)(2,1)S(1)}, bf16[4,1,128,256]{3,2,1,0:T(8,128)(2,1)S(1)}, u32[]{:S(2)}, u32[]{:S(2)}) collective-permute-start(bf16[4,1,128,256]{3,2,1,0:T(8,128)(2,1)S(1)} %get-tuple-element.144), channel_id=1, source_target_pairs={{1,0},{2,1},{3,2},{4,3},{5,4},{6,5},{7,6},{9,8},{10,9},{11,10},{12... | collective-permute-start | bytes 786440 | tf_op jit(solution)/shard_map/ppermute | solution.py:28
  609.9 2.8 copy-start.3
  612.7 2.0 copy-start.7
  619.9 1.2 copy-start.6
Sparse Core Ops, SparseCore 0:
  13.6 130.9 all-gather.4
  156.2 73.0 all-gather.6
  231.8 70.8 all-gather.8
  426.1 128.5 reduce-scatter.1
where the time goes:
time: 641 us; the launch traced here: 629 us
  waiting for transfers between devices  362 us (56%)
  matrix products  120 us (19%)
  local copies, waits for them, and re-layouts  91.5 us (14%)
  starting transfers between devices  25.4 us (4%)
  between operations  15.3 us (2%)
  other arithmetic  13.2 us (2%)
    reduce_scatter x1, waiting for transfers between devices, per_device(): lax.psum_scatter(jnp.dot(attended, w_out, preferred_element_type=jnp.floa...  127 us
    all_gather x1, waiting for transfers between devices, per_device(): lax.all_gather(normed, 'sp', axis=0, tiled=True)  124 us
    all_gather x1, waiting for transfers between devices, per_device(): lax.all_gather(keys, 'grp', axis=0, tiled=True)  52.4 us
    dot_general x17, matrix products, step(): jnp.einsum('hqk,khd->hqd', weights, value_block, preferred_element_type=j...  47.5 us
    all_gather x1, waiting for transfers between devices, per_device(): lax.all_gather(values, 'grp', axis=0, tiled=True)  45.9 us
    unnamed x42, local copies, waits for them, and re-layouts  45.6 us
    dot_general x17, matrix products, step(): jnp.einsum('qhd,khd->hqk', queries, key_block, preferred_element_type=jnp...  42.8 us
    while x4, local copies, waits for them, and re-layouts, absorb(): carry, unused = lax.scan(step, carry, (key_blocks, value_blocks))  27.6 us
  transfers between devices with their start and end apart: 10, of which 9 were waited for; matrix products, arithmetic and copies ran while one was open for 9% of the time, Pallas kernels for 0%

commit v1 on v0

v1 whole, which is shorter than its diff:
```python
import math

import jax
import jax.numpy as jnp
from jax import lax
from jax.experimental import pallas as pl
from jax.experimental.pallas import tpu as pltpu
from jax.sharding import PartitionSpec as P

HD = 128
EPS = 1e-06
MESH = pl.DeviceIdType.MESH
F32 = jnp.float32
BF16 = jnp.bfloat16


def layer_norm(values):
    middle = jnp.mean(values, axis=-1, keepdims=True)
    centered = values - middle
    spread = jnp.mean(centered * centered, axis=-1, keepdims=True)
    return centered * lax.rsqrt(spread + EPS)


def rms_scale(values, gain):
    return values * lax.rsqrt(jnp.mean(values * values, axis=-1, keepdims=True) + EPS) * gain


class Ring:
    def __init__(self, at, before, after, mate, piece, half, send, recv):
        self.at = at
        self.before, self.after, self.mate = before, after, mate
        self.piece, self.half = piece, half
        self.send, self.recv = send, recv

    def copy(self, i, slot, j, device):
        return pltpu.make_async_remote_copy(
            src_ref=slot,
            dst_ref=slot,
            send_sem=self.send.at[i, j],
            recv_sem=self.recv.at[i, j],
            device_id=device,
            device_id_type=MESH,
        )

    def place(self, step):
        return lax.rem(self.at + step, 4)

    def out(self, i, j):
        if j in (0, 1, 2):
            return self.copy(i, self.piece(i, self.at), j, (self.after, self.before, self.mate)[j])
        if j == 3:
            return self.copy(i, self.half(i, self.place(3), 0), j, self.after)
        if j == 5:
            return self.copy(i, self.half(i, self.place(1), 1), j, self.before)
        return self.copy(i, self.piece(i, self.place({4: 3, 6: 1, 7: 2}[j])), j, self.mate)

    def start(self, i, mate):
        for j in (0, 1, 2) if mate else (0, 1):
            self.out(i, j).start()

    def landed(self, i, j, mate_piece=None):
        slot = {
            0: lambda: self.piece(i, self.place(3)),
            1: lambda: self.piece(i, self.place(1)),
            3: lambda: self.half(i, self.place(2), 0),
            5: lambda: self.half(i, self.place(2), 1),
        }
        if j in slot:
            where = slot[j]()
        else:
            where = mate_piece(i, self.place({2: 0, 4: 3, 6: 1, 7: 2}[j]))
        self.copy(i, where, j, self.after).wait_recv()

    def forward(self, i, mate):
        self.landed(i, 0)
        self.out(i, 3).start()
        self.landed(i, 1)
        self.out(i, 5).start()
        if mate:
            self.out(i, 4).start()
            self.out(i, 6).start()

    def opposite(self, i, mate):
        self.landed(i, 3)
        self.landed(i, 5)
        if mate:
            self.out(i, 7).start()

    def finish(self, i, js):
        for j in js:
            self.out(i, j).wait_send()


def block_kernel(
    x_ref,
    shift_ref,
    scale_ref,
    gate_ref,
    w_qkv_ref,
    text_k_ref,
    text_v_ref,
    q_gain_ref,
    k_gain_ref,
    w_out_ref,
    w_final_ref,
    out_ref,
    lat_ref,
    tokens,
    weights,
    qkv,
    stage,
    stage_far,
    acc,
    totals,
    w_out,
    att_out,
    att,
    local_sem,
    copy_sem,
    wx_send,
    wx_recv,
    w_send,
    w_recv,
    t_send,
    t_recv,
    ox_send,
    ox_recv,
    o_send,
    o_recv,
    xa_send,
    xa_recv,
    xb_send,
    xb_recv,
    kv_send,
    kv_recv,
    at_send,
    at_recv,
):
    grp, sp = lax.axis_index("grp"), lax.axis_index("sp")
    z, xh, core = lax.div(grp, 4), lax.rem(lax.div(grp, 2), 2), lax.rem(grp, 2)
    y, xl = lax.div(sp, 2), lax.rem(sp, 2)
    x = 2 * xh + xl
    rows, width = x_ref.shape
    piece_rows = width // 8
    keys_here = 4 * rows
    out_half = width // 2

    def device(dz=0, dxh=0, dcore=0, dy=0, dxl=0):
        new_grp = 4 * lax.rem(z + dz, 4) + 2 * lax.rem(xh + dxh, 2) + lax.rem(core + dcore, 2)
        new_sp = 2 * lax.rem(y + dy, 4) + lax.rem(xl + dxl, 2)
        return (new_grp, new_sp)

    own_weights = pltpu.make_async_copy(w_qkv_ref, weights.at[xl], local_sem.at[0])
    own_weights.start()
    out_rows = pl.ds(pl.multiple_of(256 * sp, 256), 256)
    own_out = pltpu.make_async_copy(w_out_ref, w_out.at[out_rows], local_sem.at[1])
    own_out.start()

    plane = [(dx, dy) for dx in range(4) for dy in range(4) if dx or dy]

    def on_plane(dx, dy):
        to_x, to_y = lax.rem(x + dx, 4), lax.rem(y + dy, 4)
        return (4 * z + 2 * lax.div(to_x, 2) + core, 2 * to_y + lax.rem(to_x, 2))

    barrier = pltpu.get_barrier_semaphore()
    partners = [on_plane(dx, dy) for dx, dy in plane]
    partners += [device(dz=1), device(dz=3), device(dcore=1)]
    for partner in partners:
        pl.semaphore_signal(barrier, inc=1, device_id=partner, device_id_type=MESH)
    pl.semaphore_wait(barrier, len(partners))

    def weight_rows(place, c):
        return pl.ds(pl.multiple_of(piece_rows * (2 * place + c), 128), piece_rows)

    def weight_piece(i, place):
        return weights.at[1 - xl, (1, 2, 0)[i], weight_rows(place, core)]

    def weight_half(i, place, h):
        start = piece_rows * (2 * place + core) + h * (piece_rows // 2)
        return weights.at[1 - xl, (1, 2, 0)[i], pl.ds(pl.multiple_of(start, 64), piece_rows // 2)]

    def weight_mate(i, place):
        return weights.at[1 - xl, (1, 2, 0)[i], weight_rows(place, 1 - core)]

    def weight_hop(i):
        part = (1, 2, 0)[i]
        return pltpu.make_async_remote_copy(
            src_ref=w_qkv_ref.at[part, weight_rows(z, core)],
            dst_ref=weights.at[xl, part, weight_rows(z, core)],
            send_sem=wx_send.at[i],
            recv_sem=wx_recv.at[i],
            device_id=device(dxl=1),
            device_id_type=MESH,
        )

    w_ring = Ring(z, device(dz=3), device(dz=1), device(dcore=1), weight_piece, weight_half, w_send, w_recv)

    def weight_landed(i):
        slot = weight_piece(i, z)
        pltpu.make_async_remote_copy(
            src_ref=slot,
            dst_ref=slot,
            send_sem=wx_send.at[i],
            recv_sem=wx_recv.at[i],
            device_id=device(dxl=1),
            device_id_type=MESH,
        ).wait_recv()

    t_ring = Ring(
        y,
        device(dy=3),
        device(dy=1),
        None,
        lambda i, place: tokens.at[place],
        lambda i, place, h: tokens.at[place, pl.ds(h * (rows // 2), rows // 2)],
        t_send,
        t_recv,
    )

    for i in range(3):
        weight_hop(i).start()
    normed = layer_norm(x_ref[...].astype(F32)) * (1.0 + scale_ref[...]) + shift_ref[...]
    tokens[y] = normed.astype(BF16)
    t_ring.start(0, False)

    def out_piece_of(i, place, c):
        start = 256 * (2 * place + (xl if i == 0 else 1 - xl))
        return w_out.at[pl.ds(pl.multiple_of(start, 256), 256), pl.ds(pl.multiple_of(out_half * c, 128), out_half)]

    def out_half_of(i, place, h):
        start = 256 * (2 * place + (xl if i == 0 else 1 - xl)) + 128 * h
        return w_out.at[pl.ds(pl.multiple_of(start, 128), 128), pl.ds(pl.multiple_of(out_half * core, 128), out_half)]

    def out_piece(i, place):
        return out_piece_of(i, place, core)

    def out_mate(i, place):
        return out_piece_of(i, place, 1 - core)

    o_ring = Ring(y, device(dy=3), device(dy=1), device(dcore=1), out_piece, out_half_of, o_send, o_recv)

    def out_hop(slot):
        return pltpu.make_async_remote_copy(
            src_ref=slot,
            dst_ref=slot,
            send_sem=ox_send.at[0],
            recv_sem=ox_recv.at[0],
            device_id=device(dxl=1),
            device_id_type=MESH,
        )

    scale = HD ** (-0.5) / math.log(2.0)
    q_gain = q_gain_ref[...] * scale
    k_gain = k_gain_ref[...]
    block = 2 * z + core

    def finish_part(part, values):
        if part == 2:
            return values.astype(BF16)
        return rms_scale(values, q_gain if part == 0 else k_gain).astype(BF16)

    def near_copy(j, place, near):
        here = pl.ds(pl.multiple_of(place * rows, rows), rows)
        if near:
            return pltpu.make_async_copy(stage.at[j, xh], qkv.at[block, x, :, here], copy_sem.at[j])
        return pltpu.make_async_remote_copy(
            src_ref=stage.at[j, 1 - xh],
            dst_ref=qkv.at[block, x, :, here],
            send_sem=xa_send.at[j],
            recv_sem=xa_recv.at[j],
            device_id=device(dxh=1),
            device_id_type=MESH,
        )

    def near_heads(j, place):
        for part in (1, 2, 0):
            made = jnp.dot(tokens[place], weights[xl, part], preferred_element_type=F32)
            for head in range(2):
                stage[j, head, part] = finish_part(part, made[:, head * HD : (head + 1) * HD])
        for near in (False, True):
            near_copy(j, place, near).start()

    def far_copy(i, a):
        part = (1, 2, 0)[i]
        head = lax.rem(xh + a, 2)
        return pltpu.make_async_remote_copy(
            src_ref=stage_far.at[part, head],
            dst_ref=qkv.at[block, x, part],
            send_sem=xb_send.at[a, i],
            recv_sem=xb_recv.at[a, i],
            device_id=device(dxh=a, dxl=1),
            device_id_type=MESH,
        )

    def far_heads(i):
        part = (1, 2, 0)[i]
        all_tokens = tokens[...].reshape(4 * rows, width)
        made = jnp.dot(all_tokens, weights[1 - xl, part], preferred_element_type=F32)
        for head in range(2):
            stage_far[part, head] = finish_part(part, made[:, head * HD : (head + 1) * HD])
        for a in range(2):
            far_copy(i, a).start()

    places = [y, lax.rem(y + 3, 4), lax.rem(y + 1, 4), lax.rem(y + 2, 4)]
    weight_landed(0)
    w_ring.start(0, True)
    own_weights.wait()
    near_heads(0, places[0])
    weight_landed(1)
    w_ring.start(1, True)
    w_ring.forward(0, True)
    weight_landed(2)
    w_ring.start(2, True)
    own_out.wait()
    out_hop(out_piece(0, y)).start()
    w_ring.forward(1, True)
    t_ring.forward(0, False)
    w_ring.opposite(0, True)
    w_ring.forward(2, True)
    near_heads(1, places[1])
    near_heads(2, places[2])
    w_ring.opposite(1, True)
    w_ring.opposite(2, True)
    t_ring.opposite(0, False)
    o_ring.start(0, False)
    out_hop(out_piece(1, y)).wait_recv()
    o_ring.start(1, True)
    near_heads(3, places[3])
    for i in range(3):
        for j in (2, 4, 6, 7):
            w_ring.landed(i, j, weight_mate)
        far_heads(i)

    sources = [2 * lax.rem(xh + a, 2) + lax.rem(xl + b, 2) for b in range(2) for a in range(2)]

    def kv_piece_of(i, place, c):
        return qkv.at[2 * place + c, sources[i], pl.ds(1, 2)]

    def kv_piece(i, place):
        return kv_piece_of(i, place, core)

    def kv_half(i, place, h):
        return qkv.at[2 * place + core, sources[i], 1 + h]

    def kv_mate(i, place):
        return kv_piece_of(i, place, 1 - core)

    kv_ring = Ring(z, device(dz=3), device(dz=1), device(dcore=1), kv_piece, kv_half, kv_send, kv_recv)

    for j in range(4):
        near_copy(j, places[j], True).wait()
    kv_ring.start(0, True)
    for j in range(4):
        here = pl.ds(pl.multiple_of(places[j] * rows, rows), rows)
        slot = qkv.at[block, sources[1], :, here]
        pltpu.make_async_remote_copy(
            src_ref=slot,
            dst_ref=slot,
            send_sem=xa_send.at[j],
            recv_sem=xa_recv.at[j],
            device_id=device(dxh=1),
            device_id_type=MESH,
        ).wait_recv()
    kv_ring.start(1, True)
    for a in range(2):
        for i in range(3):
            slot = qkv.at[block, sources[2 + a], (1, 2, 0)[i]]
            pltpu.make_async_remote_copy(
                src_ref=slot,
                dst_ref=slot,
                send_sem=xb_send.at[a, i],
                recv_sem=xb_recv.at[a, i],
                device_id=device(dxl=1),
                device_id_type=MESH,
            ).wait_recv()
        kv_ring.start(2 + a, True)

    q_tile = 2 * keys_here

    def attend(first, keys, values, tile):
        here = pl.ds(tile * q_tile, q_tile)
        queries = qkv[block, pl.ds(2 * tile, 2), 0].reshape(q_tile, HD)
        scores = lax.dot_general(queries, keys, (((1,), (1,)), ((), ())), preferred_element_type=F32)
        weight = jnp.exp2(scores).astype(BF16)
        added = weight[:, :HD].astype(F32)
        for k in range(1, keys.shape[0] // HD):
            added = added + weight[:, k * HD : (k + 1) * HD].astype(F32)
        product = jnp.dot(weight, values, preferred_element_type=F32)
        if first:
            totals[here] = added
            acc[here] = product
        else:
            totals[here] += added
            acc[here] += product

    for tile in range(2):
        attend(True, text_k_ref[...], text_v_ref[...], tile)

    def step(t, carry):
        def at(n, work):
            @pl.when(t == n)
            def _():
                work()

        def mates(i, j):
            return lambda: kv_ring.landed(i, j, kv_mate)

        at(0, lambda: o_ring.forward(0, True))
        at(2, lambda: kv_ring.forward(0, True))
        at(2, mates(0, 2))
        at(2, mates(1, 2))
        at(3, mates(2, 2))
        at(3, mates(3, 2))
        at(4, lambda: kv_ring.forward(1, True))
        at(5, lambda: o_ring.forward(1, True))
        at(6, mates(0, 4))
        at(6, mates(1, 4))
        at(6, lambda: kv_ring.forward(2, True))
        at(7, mates(0, 6))
        at(7, mates(1, 6))
        at(8, lambda: kv_ring.forward(3, True))
        at(9, lambda: o_ring.opposite(0, True))
        at(9, lambda: kv_ring.opposite(0, True))
        at(10, mates(2, 4))
        at(10, mates(3, 4))
        at(10, lambda: kv_ring.opposite(1, True))
        at(11, mates(2, 6))
        at(11, mates(3, 6))
        at(11, lambda: kv_ring.opposite(2, True))
        at(12, lambda: kv_ring.opposite(3, True))
        at(12, lambda: o_ring.opposite(1, True))
        at(13, mates(0, 7))
        at(13, mates(1, 7))
        at(15, mates(2, 7))
        at(15, mates(3, 7))
        late = t >= 12
        wide = lax.rem(t, 4)
        place = jnp.where(t < 4, 0, jnp.where(late, 2, jnp.where(lax.rem(t, 2) == 0, 3, 1)))
        other = jnp.where(t < 4, lax.div(t, 2), jnp.where(late, lax.rem(t, 2), lax.div(wide, 2)))
        pair = jnp.where(t < 4, lax.rem(t, 2), jnp.where(late, lax.div(t - 12, 2), lax.div(t - 4, 4)))
        b = 2 * lax.rem(z + place, 4) + lax.rem(core + other, 2)
        first = 2 * xh + lax.rem(xl + pair, 2)
        second = 2 * (1 - xh) + lax.rem(xl + pair, 2)
        keys = jnp.concatenate([qkv[b, first, 1], qkv[b, second, 1]], axis=0)
        values = jnp.concatenate([qkv[b, first, 2], qkv[b, second, 2]], axis=0)
        for tile in range(2):
            attend(False, keys, values, tile)
        return carry

    lax.fori_loop(0, 16, step, 0)

    head = 2 * sp + xh

    def attended_copy(n):
        dx, dy = plane[n]
        source = 4 * lax.rem(x + dx, 4) + lax.rem(y + dy, 4)
        return pltpu.make_async_remote_copy(
            src_ref=att_out.at[source],
            dst_ref=att.at[:, pl.ds(pl.multiple_of(head * HD, HD), HD)],
            send_sem=at_send.at[n],
            recv_sem=at_recv.at[n],
            device_id=on_plane(dx, dy),
            device_id_type=MESH,
        )

    for s in range(4):
        here = pl.ds(s * keys_here, keys_here)
        total = jnp.sum(totals[here], axis=-1, keepdims=True)
        att_out[pl.ds(4 * s, 4)] = (acc[here] / total).astype(BF16).reshape(4, rows, HD)
    for n in range(len(plane)):
        attended_copy(n).start()
    att[:, pl.ds(pl.multiple_of(head * HD, HD), HD)] = att_out[4 * x + y]

    for j in (4, 6, 7):
        o_ring.landed(0, j, out_mate)
    for j in (2, 4, 6, 7):
        o_ring.landed(1, j, out_mate)
    for n, (dx, dy) in enumerate(plane):
        from_x, from_y = lax.rem(x + 4 - dx, 4), lax.rem(y + 4 - dy, 4)
        from_head = 2 * (2 * from_y + lax.rem(from_x, 2)) + lax.div(from_x, 2)
        slot = att.at[:, pl.ds(pl.multiple_of(from_head * HD, HD), HD)]
        pltpu.make_async_remote_copy(
            src_ref=slot,
            dst_ref=slot,
            send_sem=at_send.at[n],
            recv_sem=at_recv.at[n],
            device_id=on_plane(dx, dy),
            device_id_type=MESH,
        ).wait_recv()

    def project(n, carry):
        columns = pl.ds(pl.multiple_of(n * 512, 512), 512)
        proj = jnp.dot(att[...], w_out[:, columns], preferred_element_type=F32)
        out_ref[:, columns] = (x_ref[:, columns].astype(F32) + gate_ref[:, columns] * proj).astype(BF16)
        return carry

    lax.fori_loop(0, width // 512, project, 0)
    final = layer_norm(out_ref[...].astype(F32)).astype(BF16)
    latent = lax.dot_general(final, w_final_ref[...], (((1,), (1,)), ((), ())), preferred_element_type=F32)
    latent = latent.astype(BF16)

    frames, breadth = 2, rows // 2
    patch = latent.shape[1] // 2
    row, col = (lax.broadcasted_iota(jnp.int32, (rows, rows), d) for d in (0, 1))
    feature, lane = (lax.broadcasted_iota(jnp.int32, (2 * patch, HD), d) for d in (0, 1))
    same = lax.div(row, breadth) == lax.div(col, breadth)
    views = [jnp.zeros((rows, HD), F32)] * 2
    for d in range(3):
        shift = ((col == row + (d - 1)) & same).astype(F32).astype(BF16)
        moved = jnp.dot(shift, latent, preferred_element_type=F32).astype(BF16)
        for p in range(2):
            spread = (feature - p * patch == lane - d * patch) & (lane >= d * patch) & (lane < (d + 1) * patch)
            views[p] += jnp.dot(moved, spread.astype(F32).astype(BF16), preferred_element_type=F32)
    for p in range(2):
        for f in range(frames):
            lat_ref[f, p] = views[p][f * breadth : (f + 1) * breadth].astype(BF16)

    for i in range(3):
        weight_hop(i).wait_send()
        w_ring.finish(i, range(8))
        for a in range(2):
            far_copy(i, a).wait_send()
    t_ring.finish(0, (0, 1, 3, 5))
    out_hop(out_piece(0, y)).wait_send()
    o_ring.finish(0, (0, 1, 3, 4, 5, 6, 7))
    o_ring.finish(1, range(8))
    for j in range(4):
        near_copy(j, places[j], False).wait_send()
        kv_ring.finish(j, range(8))
    for n in range(len(plane)):
        attended_copy(n).wait_send()


def decode_kernel(lat_ref, w_in_ref, w_mid_ref, clip_ref, out_ref, window, w_taps, planes, direct, send, recv):
    grp, sp = lax.axis_index("grp"), lax.axis_index("sp")
    slabs, tiles = lax.axis_size("grp"), lax.axis_size("sp")
    breadth = lat_ref.shape[1] // 2
    cv = w_in_ref.shape[-1]
    ways = [(dg, ds) for dg in range(3) for ds in (-1, 0, 1) if dg or ds]

    def inside(dg, ds):
        g, s = grp + dg, sp + ds
        return (g >= 0) & (g < slabs) & (s >= 0) & (s < tiles)

    barrier = pltpu.get_barrier_semaphore()
    count = 0
    for dg in (-2, -1, 0, 1, 2):
        for ds in (-1, 0, 1):
            if dg or ds:
                there = inside(dg, ds)

                @pl.when(there)
                def _():
                    pl.semaphore_signal(barrier, inc=1, device_id=(grp + dg, sp + ds), device_id_type=MESH)

                count = count + jnp.where(there, 1, 0)

    @pl.when(sp == 0)
    def _():
        window[:, 0 : 2 * breadth] = jnp.zeros((6, 2 * breadth, HD), BF16)

    @pl.when(sp == tiles - 1)
    def _():
        window[:, 4 * breadth :] = jnp.zeros((6, 2 * breadth, HD), BF16)

    for first in (0, 1):

        @pl.when(grp == first)
        def _():
            window[0 : 4 - 2 * first] = jnp.zeros((4 - 2 * first, 6 * breadth, HD), BF16)

    pl.semaphore_wait(barrier, count)

    def halo_copy(n):
        dg, ds = ways[n]
        return pltpu.make_async_remote_copy(
            src_ref=lat_ref,
            dst_ref=window.at[pl.ds(4 - 2 * dg, 2), pl.ds(2 * breadth * (1 - ds), 2 * breadth)],
            send_sem=send.at[n],
            recv_sem=recv.at[n],
            device_id=(grp + dg, sp + ds),
            device_id_type=MESH,
        )

    for n, (dg, ds) in enumerate(ways):

        @pl.when(inside(dg, ds))
        def _():
            halo_copy(n).start()

    window[pl.ds(4, 2), pl.ds(2 * breadth, 2 * breadth)] = lat_ref[...]

    w_taps[...] = jnp.zeros_like(w_taps)
    ch = w_in_ref.shape[3]
    for kt in range(3):
        for kr in range(3):
            for d in range(3):
                for q in range(2):
                    for q_out in range(2):
                        kc = 2 * (d - 1) + q - q_out + 1
                        if 0 <= kc < 3:
                            w_taps[3 * kt + kr, pl.ds((2 * d + q) * ch, ch), pl.ds(cv * q_out, cv)] = w_in_ref[kt, kr, kc]

    first_frame = 2 * grp
    starts = []
    for f in range(4):
        clip = clip_ref[jnp.maximum(first_frame - 2 + f, 0)]
        start = 0
        for j in range(clip_ref.shape[0]):
            start = start + jnp.where(clip_ref[j] < clip, 1, 0)
        starts.append(start)

    for n, (dg, ds) in enumerate(ways):

        @pl.when(inside(-dg, -ds))
        def _():
            halo_copy(n).wait_recv()

    def frame_at(f, kt, lowest, size):
        index = jnp.maximum(first_frame - 2 + f - kt, starts[f]) - (first_frame - lowest)
        return jnp.clip(index, 0, size - 1)

    tile = lax.broadcasted_iota(jnp.int32, (4 * breadth, 1), 0)
    outside = ((tile < breadth) & (sp == 0)) | ((tile >= 3 * breadth) & (sp == tiles - 1))
    row, col = (lax.broadcasted_iota(jnp.int32, (4 * breadth, 4 * breadth), d) for d in (0, 1))
    same = lax.div(row, breadth) == lax.div(col, breadth)
    left = ((col == row - 1) & same).astype(F32).astype(BF16)
    right = ((col == row + 1) & same).astype(F32).astype(BF16)
    for f in range(4):
        total = jnp.zeros((4 * breadth, 2 * cv), F32)
        for kt in range(3):
            index = frame_at(f, kt, 4, 6)
            for kr in range(3):
                seen = window[index, pl.ds(kr * breadth, 4 * breadth)]
                total = total + jnp.dot(seen, w_taps[3 * kt + kr], preferred_element_type=F32)
        if f >= 2:
            direct[f - 2] = total[breadth : 3 * breadth]
        act = jnp.where(outside, 0.0, total / (1.0 + jnp.exp(-total))).astype(BF16)
        even, odd = act[:, :cv], act[:, cv:]
        planes[0, f] = jnp.dot(left, odd, preferred_element_type=F32).astype(BF16)
        planes[1, f] = even
        planes[2, f] = odd
        planes[3, f] = jnp.dot(right, even, preferred_element_type=F32).astype(BF16)

    mixed = jnp.zeros((8 * breadth, cv), F32)
    for kt in range(3):
        index = [frame_at(2 + f, kt, 2, 4) for f in range(2)]
        for kr in range(3):
            rows = pl.ds(kr * breadth, 2 * breadth)
            seen = [
                jnp.concatenate([planes[q + kc, index[f], rows] for kc in range(3)], axis=1)
                for f in range(2)
                for q in range(2)
            ]
            mixed = mixed + jnp.dot(jnp.concatenate(seen, axis=0), w_mid_ref[3 * kt + kr], preferred_element_type=F32)

    row, col = (lax.broadcasted_iota(jnp.int32, (2 * breadth, 2 * breadth), d) for d in (0, 1))
    woven = (col == lax.div(row, 2) + breadth * lax.rem(row, 2)).astype(F32).astype(BF16)
    for f in range(2):
        for r in range(2):
            pair = []
            for q in range(2):
                start = (2 * f + q) * 2 * breadth + r * breadth
                added = mixed[start : start + breadth] + direct[f, r * breadth : (r + 1) * breadth, q * cv : (q + 1) * cv]
                pair.append(added.astype(BF16))
            out_ref[f, r] = jnp.dot(woven, jnp.concatenate(pair, axis=0), preferred_element_type=F32).astype(BF16)

    for n, (dg, ds) in enumerate(ways):

        @pl.when(inside(dg, ds))
        def _():
            halo_copy(n).wait_send()


def per_device(
    image_tokens,
    text_tokens,
    mod_shift,
    mod_scale,
    mod_gate,
    w_qkv,
    w_text_kv,
    q_gain,
    k_gain,
    text_gain,
    w_out,
    w_final,
    w_conv_in,
    w_conv_mid,
    clip_ids,
):
    slab, patch_rows, breadth, width = image_tokens.shape
    rows = slab * patch_rows * breadth
    inner_here = w_qkv.shape[2]
    inner = w_out.shape[0] * lax.axis_size("sp")
    cv = w_conv_in.shape[-1]
    head_here = lax.rem(lax.div(lax.axis_index("grp"), 2), 2)
    text_count = text_tokens.shape[0]
    text_normed = layer_norm(text_tokens.astype(F32)).astype(BF16)
    w_text = lax.dynamic_slice_in_dim(w_text_kv, head_here * HD, HD, axis=2)
    text_projected = jnp.dot(text_normed, w_text.reshape(width, 2 * HD), preferred_element_type=F32)
    text_keys = rms_scale(text_projected[:, :HD], text_gain).astype(BF16)
    text_values = text_projected[:, HD:].astype(BF16)

    vmem = pl.BlockSpec(memory_space=pltpu.VMEM)
    anywhere = pl.BlockSpec(memory_space=pl.ANY)
    dma = pltpu.SemaphoreType.DMA
    block_flat, views = pl.pallas_call(
        block_kernel,
        out_shape=(
            jax.ShapeDtypeStruct((rows, width), BF16),
            jax.ShapeDtypeStruct((slab, 2, breadth, HD), BF16),
        ),
        in_specs=[vmem] * 4 + [anywhere] + [vmem] * 4 + [anywhere, vmem],
        out_specs=(vmem, vmem),
        scratch_shapes=[
            pltpu.VMEM((4, rows, width), BF16),
            pltpu.VMEM((2, 3, width, inner_here), BF16),
            pltpu.VMEM((8, 4, 3, 4 * rows, HD), BF16),
            pltpu.VMEM((4, 2, 3, rows, HD), BF16),
            pltpu.VMEM((3, 2, 4 * rows, HD), BF16),
            pltpu.VMEM((16 * rows, HD), F32),
            pltpu.VMEM((16 * rows, HD), F32),
            pltpu.VMEM((inner, width), BF16),
            pltpu.VMEM((16, rows, HD), BF16),
            pltpu.VMEM((rows, inner), BF16),
            dma((2,)),
            dma((4,)),
            dma((3,)),
            dma((3,)),
            dma((3, 8)),
            dma((3, 8)),
            dma((1, 8)),
            dma((1, 8)),
            dma((1,)),
            dma((1,)),
            dma((2, 8)),
            dma((2, 8)),
            dma((4,)),
            dma((4,)),
            dma((2, 3)),
            dma((2, 3)),
            dma((4, 8)),
            dma((4, 8)),
            dma((15,)),
            dma((15,)),
        ],
        compiler_params=pltpu.CompilerParams(
            collective_id=0, has_side_effects=True, vmem_limit_bytes=58 * 1024 * 1024
        ),
    )(
        image_tokens.reshape(rows, width),
        mod_shift.reshape(1, width),
        mod_scale.reshape(1, width),
        mod_gate.reshape(1, width),
        jnp.transpose(w_qkv, (1, 0, 2)),
        text_keys,
        text_values,
        q_gain.reshape(1, HD),
        k_gain.reshape(1, HD),
        w_out,
        jnp.transpose(w_final),
    )

    decoded = pl.pallas_call(
        decode_kernel,
        out_shape=jax.ShapeDtypeStruct((slab, 2 * patch_rows, 2 * breadth, cv), BF16),
        in_specs=[vmem] * 3 + [pl.BlockSpec(memory_space=pltpu.SMEM)],
        out_specs=vmem,
        scratch_shapes=[
            pltpu.VMEM((6, 6 * breadth, HD), BF16),
            pltpu.VMEM((9, HD, 2 * cv), BF16),
            pltpu.VMEM((4, 4, 4 * breadth, cv), BF16),
            pltpu.VMEM((2, 2 * breadth, 2 * cv), F32),
            dma((8,)),
            dma((8,)),
        ],
        compiler_params=pltpu.CompilerParams(
            collective_id=1, has_side_effects=True, vmem_limit_bytes=32 * 1024 * 1024
        ),
    )(
        views.reshape(slab, 2 * breadth, HD),
        w_conv_in,
        w_conv_mid.reshape(9, 3 * cv, cv),
        clip_ids,
    )
    return (block_flat.reshape(slab, patch_rows, breadth, width), decoded)


def solution(mesh):
    return jax.shard_map(
        per_device,
        mesh=mesh,
        in_specs=(
            P("grp", "sp", None, None),
            P(),
            P(),
            P(),
            P(),
            P(None, None, "sp"),
            P(None, None, "sp"),
            P(),
            P(),
            P(),
            P("sp", None),
            P(),
            P(),
            P(),
            P(),
        ),
        out_specs=(P("grp", "sp", None, None), P("grp", "sp", None, None)),
        check_vma=False,
    )
```

time: 641 us -> 149 us (0.23); the launches traced: 629 us -> 149 us
  waiting for transfers between devices: 362 us -> 0 us
  Pallas kernels: 0 us -> 136 us
  matrix products: 120 us -> 0.7 us
  local copies, waits for them, and re-layouts: 91.5 us -> 6.24 us
  starting transfers between devices: 25.4 us -> 0 us
  between operations: 15.3 us -> 0.78 us
  other arithmetic: 13.2 us -> 4.67 us
    all_gather x3 -> x0, waiting for transfers between devices: 223 us -> none  [the longest x1 124 us: per_device(): lax.all_gather(normed, 'sp', axis=0, tiled=True)]
    pallas_call x0 -> x2, Pallas kernels: none -> 136 us  [the longest x1 113 us: per_device(): pl.pallas_call(block_kernel, out_shape=(jax.ShapeDtypeStruct((rows, width...]
    reduce_scatter x1 -> x0, waiting for transfers between devices: 127 us -> none  [per_device(): lax.psum_scatter(jnp.dot(attended, w_out, preferred_element_type=jnp.floa...]
    dot_general x92 -> x1, matrix products: 120 us -> 0.7 us  [per_device(): jnp.dot(text_normed, w_text.reshape(width, 2 * HD), preferred_element_typ...]
    unnamed x42 -> x18, local copies, waits for them, and re-layouts: 45.6 us -> 4.45 us
    while x4 -> x0, local copies, waits for them, and re-layouts: 27.6 us -> none  [absorb(): carry, unused = lax.scan(step, carry, (key_blocks, value_blocks))]
    ppermute x6 -> x0, starting transfers between devices: 25.3 us -> none  [the longest x2 12.7 us: passed_along(): lax.ppermute(value, axis, [(source, source + steps) for source in range(f...]
    ppermute x6 -> x0, waiting for transfers between devices: 12.5 us -> none  [the longest x2 5.82 us: with_halo(): after = lax.ppermute(first, axis, down)]
  transfers between devices with their start and end apart: 10 -> 0, of which waited for: 9 -> 0; matrix products, arithmetic and copies ran while one was open for 9% -> 0% of each run, Pallas kernels for 0% -> 0%
where the time goes in v1:
time: 149 us
  Pallas kernels  136 us (91%)
  local copies, waits for them, and re-layouts  6.24 us (4%)
  other arithmetic  4.67 us (3%)
    pallas_call x1, Pallas kernels, per_device(): pl.pallas_call(block_kernel, out_shape=(jax.ShapeDtypeStruct((rows, width...  113 us
    pallas_call x1, Pallas kernels, per_device(): pl.pallas_call(decode_kernel, out_shape=jax.ShapeDtypeStruct((slab, 2 * p...  23.8 us
    unnamed x18, local copies, waits for them, and re-layouts  4.45 us

profile of v1, /device:TPU:41, one launch (start us, length us, event | category | flops | bytes accessed | tf_op | source)
XLA Modules:
  0.0 148.7 jit_solution(6351273535622436889)
XLA Ops:
  0.6 0.0 copy-start
  0.7 0.0 copy-start.5
  0.7 1.8 %convert_reduce_fusion = f32[256]{0:T(256)S(1)} fusion(bf16[256,3072]{1,0:T(8,128)(2,1)} %param.16), kind=kLoop, calls=%fused_computation.1 | loop fusion | flops 1572608 | bytes 1573888 | tf_op jit(solution)/shard_map/reduce_sum | solution.py:18
  2.5 2.0 %fusion.2 = f32[256]{0:T(256)S(1)} fusion(bf16[256,3072]{1,0:T(8,128)(2,1)} %param.16, f32[256]{0:T(256)S(1)} %broadcast_multiply_fusion), kind=kLoop, calls=%fused_computation.4 | loop fusion | flops 3145472 | bytes 1574912 | tf_op jit(solution)/shard_map/reduce_sum | solution.py:20
  4.5 0.0 copy-done
  4.5 1.1 constant_dynamic-slice_fusion
  5.7 0.0 copy-start.7
  5.7 0.0 copy-done.5
  5.7 0.7 fusion.4
  6.4 0.1 multiply_reduce_fusion
  6.5 0.0 copy-done.7
  6.5 0.7 multiply_convert_fusion.text_k_ref
  7.3 0.6 slice.14.text_v_ref
  7.9 0.0 copy-start.2
  7.9 0.0 copy-start.4
  7.9 112.5 %shard_map.158 = (bf16[128,3072]{1,0:T(8,128)(2,1)}, bf16[2,2,64,128]{3,2,1,0:T(8,128)(2,1)}) custom-call(bf16[128,3072]{1,0:T(8,128)(2,1)} %bitcast.21, f32[1,3072]{1,0:T(1,128)} %bitcast.24, f32[1,3072]{1,0:T(1,128)} %bitcast.25, f32[1,3072]{1,0:T(1,128)} %bitcast.26, bf16[3,3072,256]{2,1,0:T(8,128)(2,1)} %bitcast.19, ...), custom_call_target="tpu_custom_call" | custom-call | tf_op jit(solution)/shard_map/pallas_call | solution.py:708
  120.4 0.0 copy-done.2
  120.5 0.0 copy-done.4
  120.5 0.0 copy-start.1
  120.5 2.0 %copy-done.1 = bf16[3,3,3,256,256]{4,3,2,1,0:T(8,128)(2,1)S(1)} copy-done((bf16[3,3,3,256,256]{4,3,2,1,0:T(8,128)(2,1)S(1)}, bf16[3,3,3,256,256]{4,3,2,1,0:T(8,128)(2,1)}, u32[]{:S(2)}) %copy-start.1) | copy-done | bytes 3538968
  122.5 0.0 copy-start.3
  122.5 0.8 copy-done.3
  123.3 0.0 copy-start.6
  123.3 23.8 %shard_map.159 = bf16[2,2,128,256]{3,2,1,0:T(8,128)(2,1)S(1)} custom-call(bf16[2,128,128]{2,1,0:T(8,128)(2,1)S(1)} %bitcast.18, bf16[3,3,3,16,256]{4,3,2,1,0:T(8,128)(2,1)S(1)} %copy-done.2, bf16[9,768,256]{2,1,0:T(8,128)(2,1)S(1)} %bitcast.17, s32[32]{0:T(128)S(1)} %copy-done.4), custom_call_target="tpu_custom_call" | custom-call | tf_op jit(solution)/shard_map/pallas_call | solution.py:765
  147.1 0.0 copy-done.6
  147.1 0.9 copy.28
  148.0 0.7 copy.29
  (3 shorter events, 0.0 us)
Async XLA Ops:
  0.6 3.9 %copy-start = (bf16[3072,2,256]{2,1,0:T(2,128)(2,1)S(1)}, bf16[3072,2,256]{2,1,0:T(2,128)(2,1)}, u32[]{:S(2)}) copy-start(bf16[3072,2,256]{2,1,0:T(2,128)(2,1)} %param.21) | copy-start | bytes 9437188
  0.7 5.0 %copy-start.5 = (bf16[256,3072]{1,0:T(8,128)(2,1)S(1)}, bf16[256,3072]{1,0:T(8,128)(2,1)}, u32[]{:S(2)}) copy-start(bf16[256,3072]{1,0:T(8,128)(2,1)} %param.16) | copy-start | bytes 4718596
  5.7 0.9 copy-start.7
  7.9 112.5 %copy-start.2 = (bf16[3,3,3,16,256]{4,3,2,1,0:T(8,128)(2,1)S(1)}, bf16[3,3,3,16,256]{4,3,2,1,0:T(8,128)(2,1)}, u32[]{:S(2)}) copy-start(bf16[3,3,3,16,256]{4,3,2,1,0:T(8,128)(2,1)} %w_in_ref.1) | copy-start | bytes 663556
  7.9 112.5 %copy-start.4 = (s32[32]{0:T(128)S(1)}, s32[32]{0:T(128)}, u32[]{:S(2)}) copy-start(s32[32]{0:T(128)} %clip_ref.1) | copy-start | bytes 388
  120.5 2.0 %copy-start.1 = (bf16[3,3,3,256,256]{4,3,2,1,0:T(8,128)(2,1)S(1)}, bf16[3,3,3,256,256]{4,3,2,1,0:T(8,128)(2,1)}, u32[]{:S(2)}) copy-start(bf16[3,3,3,256,256]{4,3,2,1,0:T(8,128)(2,1)} %param.28) | copy-start | bytes 10616836
  122.5 0.8 copy-start.3
  123.3 23.8 %copy-start.6 = (bf16[128,3072]{1,0:T(8,128)(2,1)S(1)}, bf16[128,3072]{1,0:T(8,128)(2,1)}, u32[]{:S(2)}) copy-start(bf16[128,3072]{1,0:T(8,128)(2,1)} %get-tuple-element.4) | copy-start | bytes 2359300

commit v2 on v1

v2 whole, which is shorter than its diff:
```python
import math

import jax
import jax.numpy as jnp
from jax import lax
from jax.experimental import pallas as pl
from jax.experimental.pallas import tpu as pltpu
from jax.sharding import PartitionSpec as P

HD = 128
EPS = 1e-06
MESH = pl.DeviceIdType.MESH
F32 = jnp.float32
BF16 = jnp.bfloat16


def layer_norm(values):
    middle = jnp.mean(values, axis=-1, keepdims=True)
    centered = values - middle
    spread = jnp.mean(centered * centered, axis=-1, keepdims=True)
    return centered * lax.rsqrt(spread + EPS)


def rms_scale(values, gain):
    return values * lax.rsqrt(jnp.mean(values * values, axis=-1, keepdims=True) + EPS) * gain


class Ring:
    def __init__(self, at, before, after, mate, piece, half, send, recv):
        self.at = at
        self.before, self.after, self.mate = before, after, mate
        self.piece, self.half = piece, half
        self.send, self.recv = send, recv

    def copy(self, i, slot, j, device):
        return pltpu.make_async_remote_copy(
            src_ref=slot,
            dst_ref=slot,
            send_sem=self.send.at[i, j],
            recv_sem=self.recv.at[i, j],
            device_id=device,
            device_id_type=MESH,
        )

    def place(self, step):
        return lax.rem(self.at + step, 4)

    def out(self, i, j):
        if j in (0, 1, 2):
            return self.copy(i, self.piece(i, self.at), j, (self.after, self.before, self.mate)[j])
        if j == 3:
            return self.copy(i, self.half(i, self.place(3), 0), j, self.after)
        if j == 5:
            return self.copy(i, self.half(i, self.place(1), 1), j, self.before)
        return self.copy(i, self.piece(i, self.place({4: 3, 6: 1, 7: 2}[j])), j, self.mate)

    def start(self, i, mate):
        for j in (0, 1, 2) if mate else (0, 1):
            self.out(i, j).start()

    def landed(self, i, j, mate_piece=None):
        slot = {
            0: lambda: self.piece(i, self.place(3)),
            1: lambda: self.piece(i, self.place(1)),
            3: lambda: self.half(i, self.place(2), 0),
            5: lambda: self.half(i, self.place(2), 1),
        }
        if j in slot:
            where = slot[j]()
        else:
            where = mate_piece(i, self.place({2: 0, 4: 3, 6: 1, 7: 2}[j]))
        self.copy(i, where, j, self.after).wait_recv()

    def forward(self, i, mate):
        self.landed(i, 0)
        self.out(i, 3).start()
        self.landed(i, 1)
        self.out(i, 5).start()
        if mate:
            self.out(i, 4).start()
            self.out(i, 6).start()

    def opposite(self, i, mate):
        self.landed(i, 3)
        self.landed(i, 5)
        if mate:
            self.out(i, 7).start()

    def finish(self, i, js):
        for j in js:
            self.out(i, j).wait_send()


def whole_kernel(
    x_ref,
    shift_ref,
    scale_ref,
    gate_ref,
    w_qkv_ref,
    text_ref,
    w_text_ref,
    q_gain_ref,
    k_gain_ref,
    text_gain_ref,
    w_out_ref,
    w_final_ref,
    w_in_ref,
    w_mid_ref,
    clip_ref,
    out_ref,
    dec_ref,
    tokens,
    weights,
    qkv,
    stage,
    relay,
    acc,
    totals,
    w_out,
    att_out,
    att,
    text,
    w_text,
    text_kv,
    lat,
    window,
    w_taps,
    planes,
    direct,
    local_sem,
    copy_sem,
    wx_send,
    wx_recv,
    w_send,
    w_recv,
    t_send,
    t_recv,
    o_send,
    o_recv,
    side_send,
    side_recv,
    over_send,
    over_recv,
    far_send,
    far_recv,
    relay_send,
    relay_recv,
    near_send,
    near_recv,
    kv_send,
    kv_recv,
    at_send,
    at_recv,
    halo_send,
    halo_recv,
):
    grp, sp = lax.axis_index("grp"), lax.axis_index("sp")
    z, xh, core = lax.div(grp, 4), lax.rem(lax.div(grp, 2), 2), lax.rem(grp, 2)
    y, xl = lax.div(sp, 2), lax.rem(sp, 2)
    x = 2 * xh + xl
    rows, width = x_ref.shape
    piece_rows = width // 8
    keys_here = 4 * rows
    out_half = width // 2

    def device(dz=0, dxh=0, dcore=0, dy=0, dxl=0):
        new_grp = 4 * lax.rem(z + dz, 4) + 2 * lax.rem(xh + dxh, 2) + lax.rem(core + dcore, 2)
        new_sp = 2 * lax.rem(y + dy, 4) + lax.rem(xl + dxl, 2)
        return (new_grp, new_sp)

    def flip(a, b):
        return device(dxh=a, dxl=b)

    own_weights = pltpu.make_async_copy(w_qkv_ref, weights.at[xl], local_sem.at[0])
    own_weights.start()
    text_in = pltpu.make_async_copy(text_ref, text, local_sem.at[1])
    text_in.start()
    w_text_in = pltpu.make_async_copy(w_text_ref, w_text, local_sem.at[2])
    w_text_in.start()
    out_rows = pl.ds(pl.multiple_of(256 * sp, 256), 256)
    own_out = pltpu.make_async_copy(w_out_ref, w_out.at[out_rows], local_sem.at[3])
    own_out.start()

    plane = [(a, b, dy) for a, b in ((1, 0), (0, 1), (1, 1), (0, 0)) for dy in (2, 1, 3, 0) if a or b or dy]

    def on_plane(a, b, dy):
        return device(dxh=a, dxl=b, dy=dy)

    slabs, tiles = lax.axis_size("grp"), lax.axis_size("sp")
    ways = [(dg, ds) for dg in range(3) for ds in (-1, 0, 1) if dg or ds]

    def inside(dg, ds):
        g, s = grp + dg, sp + ds
        return (g >= 0) & (g < slabs) & (s >= 0) & (s < tiles)

    barrier = pltpu.get_barrier_semaphore()
    partners = [device(dz=1), device(dz=3), device(dcore=1)] + [on_plane(*place) for place in plane]
    for partner in partners:
        pl.semaphore_signal(barrier, inc=1, device_id=partner, device_id_type=MESH)
    expected = len(partners)
    for dg in (-2, -1, 0, 1, 2):
        for ds in (-1, 0, 1):
            if dg or ds:
                there = inside(dg, ds)

                @pl.when(there)
                def _():
                    pl.semaphore_signal(barrier, inc=1, device_id=(grp + dg, sp + ds), device_id_type=MESH)

                expected = expected + jnp.where(there, 1, 0)

    breadth = rows // 2
    zero_rows = jnp.zeros((6, 2 * breadth, HD), BF16)

    @pl.when(sp == 0)
    def _():
        window[:, 0 : 2 * breadth] = zero_rows

    @pl.when(sp == tiles - 1)
    def _():
        window[:, 4 * breadth :] = zero_rows

    for first in (0, 1):

        @pl.when(grp == first)
        def _():
            window[0 : 4 - 2 * first] = jnp.zeros((4 - 2 * first, 6 * breadth, HD), BF16)

    pl.semaphore_wait(barrier, expected)

    def weight_rows(place, c):
        return pl.ds(pl.multiple_of(piece_rows * (2 * place + c), 128), piece_rows)

    def weight_piece(i, place):
        return weights.at[1 - xl, (1, 2, 0)[i], weight_rows(place, core)]

    def weight_half(i, place, h):
        start = piece_rows * (2 * place + core) + h * (piece_rows // 2)
        return weights.at[1 - xl, (1, 2, 0)[i], pl.ds(pl.multiple_of(start, 64), piece_rows // 2)]

    def weight_mate(i, place):
        return weights.at[1 - xl, (1, 2, 0)[i], weight_rows(place, 1 - core)]

    def weight_hop(i, a, landing=False):
        part = (1, 2, 0)[i]
        start = piece_rows * (2 * z + core) + a * (piece_rows // 2)
        here = pl.ds(pl.multiple_of(start, 64), piece_rows // 2)
        slot = weights.at[1 - xl if landing else xl, part, here]
        return pltpu.make_async_remote_copy(
            src_ref=slot if landing else w_qkv_ref.at[part, here],
            dst_ref=slot,
            send_sem=wx_send.at[i, a],
            recv_sem=wx_recv.at[i, a],
            device_id=flip(a, 1),
            device_id_type=MESH,
        )

    w_ring = Ring(z, device(dz=3), device(dz=1), device(dcore=1), weight_piece, weight_half, w_send, w_recv)

    def weight_landed(i):
        for a in range(2):
            weight_hop(i, a, True).wait_recv()

    t_before, t_after, t_far = lax.rem(y + 3, 4), lax.rem(y + 1, 4), lax.rem(y + 2, 4)

    def token_copy(n, landing=False):
        place = (t_before, t_after, t_before, t_after, t_far, t_far)[n] if landing else (y, y, y, y, t_before, t_after)[n]
        h = (0, 1, 1, 0, 0, 1)[n]
        slot = tokens.at[place, pl.ds(h * (rows // 2), rows // 2)]
        return pltpu.make_async_remote_copy(
            src_ref=slot,
            dst_ref=slot,
            send_sem=t_send.at[n],
            recv_sem=t_recv.at[n],
            device_id=device(dy=(1, 3, 1, 3, 1, 3)[n]),
            device_id_type=MESH,
        )

    for i in range(3):
        for a in range(2):
            weight_hop(i, a).start()
    for h in range(2):
        here = pl.ds(h * (rows // 2), rows // 2)
        normed = layer_norm(x_ref[here].astype(F32)) * (1.0 + scale_ref[...]) + shift_ref[...]
        tokens[y, here] = normed.astype(BF16)
        token_copy(h).start()
    token_copy(2).start()
    token_copy(3).start()

    places = [y, t_before, t_after, t_far]

    def out_slot(sp_of, h, c):
        start, count = (256 * sp_of, 256) if h is None else (256 * sp_of + 128 * h, 128)
        columns = pl.ds(pl.multiple_of(out_half * c, 128), out_half)
        return w_out.at[pl.ds(pl.multiple_of(start, 128), count), columns]

    def out_piece(i, place):
        return out_slot(2 * place + xl, None, core)

    def out_mate(i, place):
        return out_slot(2 * place + xl, None, 1 - core)

    def out_half_of(i, place, h):
        return out_slot(2 * place + xl, h, core)

    o_ring = Ring(y, device(dy=3), device(dy=1), device(dcore=1), out_piece, out_half_of, o_send, o_recv)

    def side_copy(n, a, landing=False):
        slot = out_slot(2 * places[n] + (1 - xl if landing else xl), a, core)
        return pltpu.make_async_remote_copy(
            src_ref=slot,
            dst_ref=slot,
            send_sem=side_send.at[n, a],
            recv_sem=side_recv.at[n, a],
            device_id=flip(a, 1),
            device_id_type=MESH,
        )

    def over_copy(n, landing=False):
        slot = out_slot(2 * places[n] + 1 - xl, None, 1 - core if landing else core)
        return pltpu.make_async_remote_copy(
            src_ref=slot,
            dst_ref=slot,
            send_sem=over_send.at[n],
            recv_sem=over_recv.at[n],
            device_id=device(dcore=1),
            device_id_type=MESH,
        )

    def send_sideways(n):
        for a in range(2):
            side_copy(n, a).start()

    def send_over(n):
        for a in range(2):
            side_copy(n, a, True).wait_recv()
        over_copy(n).start()

    scale = HD ** (-0.5) / math.log(2.0)
    q_gain = q_gain_ref[...] * scale
    k_gain = k_gain_ref[...]
    block = 2 * z + core

    def finish_part(part, values):
        if part == 2:
            return values.astype(BF16)
        return rms_scale(values, q_gain if part == 0 else k_gain).astype(BF16)

    def token_rows(j):
        return pl.ds(pl.multiple_of(places[j] * rows, rows), rows)

    def own_copy(j):
        return pltpu.make_async_copy(stage.at[0, j, xh], qkv.at[block, x, :, token_rows(j)], copy_sem.at[j])

    def far_copy(a, j, part, landing=False):
        source = 2 * lax.rem(xh + a, 2) + 1 - xl if landing else x
        slot = qkv.at[block, source, part, token_rows(j)]
        return pltpu.make_async_remote_copy(
            src_ref=slot if landing else stage.at[1, j, lax.rem(xh + a, 2), part],
            dst_ref=slot,
            send_sem=far_send.at[a, j, part],
            recv_sem=far_recv.at[a, j, part],
            device_id=flip(a, 1),
            device_id_type=MESH,
        )

    def relay_copy(j, landing=False):
        return pltpu.make_async_remote_copy(
            src_ref=relay.at[j] if landing else stage.at[0, j, 1 - xh],
            dst_ref=relay.at[j],
            send_sem=relay_send.at[j],
            recv_sem=relay_recv.at[j],
            device_id=flip(j % 2, 1),
            device_id_type=MESH,
        )

    def near_copy(j, landing=False):
        source = 2 * (1 - xh) + xl if landing else 2 * lax.rem(xh + j % 2, 2) + 1 - xl
        slot = qkv.at[block, source, :, token_rows(j)]
        return pltpu.make_async_remote_copy(
            src_ref=slot if landing else relay.at[j],
            dst_ref=slot,
            send_sem=near_send.at[j],
            recv_sem=near_recv.at[j],
            device_id=flip(1 - j % 2, 1),
            device_id_type=MESH,
        )

    def hand_on(j):
        relay_copy(j, True).wait_recv()
        near_copy(j).start()

    def heads(b, js, parts):
        seen = jnp.concatenate([tokens[places[j]] for j in js], axis=0)
        for part in parts:
            made = jnp.dot(seen, weights[lax.rem(xl + b, 2), part], preferred_element_type=F32)
            for head in range(2):
                done = finish_part(part, made[:, head * HD : (head + 1) * HD])
                for n, j in enumerate(js):
                    stage[b, j, head, part] = done[n * rows : (n + 1) * rows]
            if b == 1:
                for j in js:
                    for a in range(2):
                        far_copy(a, j, part).start()
        if b == 0:
            for j in js:
                relay_copy(j).start()
                own_copy(j).start()

    every = (1, 2, 0)

    def far_heads(i, js):
        for j in (2, 4, 6, 7):
            w_ring.landed(i, j, weight_mate)
        heads(1, js, every[i : i + 1])

    for i in range(3):
        weight_landed(i)
        w_ring.start(i, True)
    own_weights.wait()
    heads(0, [0], every)
    w_ring.forward(0, True)
    own_out.wait()
    send_sideways(0)
    hand_on(0)

    text_in.wait()
    w_text_in.wait()
    text_normed = layer_norm(text[...].astype(F32)).astype(BF16)
    text_made = jnp.dot(text_normed, w_text[...], preferred_element_type=F32)
    text_kv[0] = rms_scale(text_made[:, :HD], text_gain_ref[...]).astype(BF16)
    text_kv[1] = text_made[:, HD:].astype(BF16)

    token_copy(0, True).wait_recv()
    token_copy(4).start()
    token_copy(1, True).wait_recv()
    token_copy(5).start()
    w_ring.forward(1, True)
    w_ring.opposite(0, True)

    w_taps[...] = jnp.zeros_like(w_taps)
    ch, cv = w_in_ref.shape[3], w_in_ref.shape[4]
    for kt in range(3):
        for kr in range(3):
            for d in range(3):
                for q in range(2):
                    for q_out in range(2):
                        kc = 2 * (d - 1) + q - q_out + 1
                        if 0 <= kc < 3:
                            first = (3 * kt + kr) * HD + (2 * d + q) * ch
                            w_taps[pl.ds(first, ch), pl.ds(cv * q_out, cv)] = w_in_ref[kt, kr, kc]

    w_ring.forward(2, True)
    token_copy(2, True).wait_recv()
    token_copy(3, True).wait_recv()
    heads(0, [1, 2], every)
    w_ring.opposite(1, True)
    far_heads(0, [0, 1, 2])
    w_ring.opposite(2, True)
    hand_on(1)
    hand_on(2)
    far_heads(1, [0, 1, 2])
    token_copy(4, True).wait_recv()
    token_copy(5, True).wait_recv()
    o_ring.start(0, False)
    heads(0, [3], every)
    heads(1, [3], (1, 2))
    hand_on(3)
    far_heads(2, [0, 1, 2, 3])

    sources = [2 * lax.rem(xh + a, 2) + lax.rem(xl + b, 2) for b in range(2) for a in range(2)]

    def kv_piece_of(i, place, c):
        return qkv.at[2 * place + c, sources[i], pl.ds(1, 2)]

    def kv_piece(i, place):
        return kv_piece_of(i, place, core)

    def kv_half(i, place, h):
        return qkv.at[2 * place + core, sources[i], 1 + h]

    def kv_mate(i, place):
        return kv_piece_of(i, place, 1 - core)

    kv_ring = Ring(z, device(dz=3), device(dz=1), device(dcore=1), kv_piece, kv_half, kv_send, kv_recv)

    for j in range(4):
        own_copy(j).wait()
    kv_ring.start(0, True)
    for j in range(4):
        near_copy(j, True).wait_recv()
    kv_ring.start(1, True)
    for a in range(2):
        for j in range(4):
            for part in range(3):
                far_copy(a, j, part, True).wait_recv()
        kv_ring.start(2 + a, True)

    for i in range(3):
        w_ring.finish(i, range(8))
    w_mid = weights.at[0, :, pl.ds(0, w_mid_ref.shape[1])]
    w_mid_in = pltpu.make_async_copy(w_mid_ref, w_mid, local_sem.at[4])
    w_mid_in.start()

    q_tile = 2 * keys_here

    def attend(first, keys, values, tile):
        here = pl.ds(tile * q_tile if isinstance(tile, int) else pl.multiple_of(tile * q_tile, q_tile), q_tile)
        one = 2 * (1 - xh) + lax.rem(xl + tile, 2)
        two = 2 * xh + lax.rem(xl + 1 - tile, 2)
        queries = jnp.concatenate([qkv[block, one, 0], qkv[block, two, 0]], axis=0)
        scores = lax.dot_general(queries, keys, (((1,), (1,)), ((), ())), preferred_element_type=F32)
        weight = jnp.exp2(scores).astype(BF16)
        added = weight[:, :HD].astype(F32)
        for k in range(1, keys.shape[0] // HD):
            added = added + weight[:, k * HD : (k + 1) * HD].astype(F32)
        product = jnp.dot(weight, values, preferred_element_type=F32)
        if first:
            totals[here] = added
            acc[here] = product
        else:
            totals[here] += added
            acc[here] += product

    for tile in range(2):
        attend(True, text_kv[0], text_kv[1], tile)

    def chunk_pair(place, other, pair):
        b = 2 * lax.rem(z + place, 4) + lax.rem(core + other, 2)
        first = 2 * xh + lax.rem(xl + pair, 2)
        second = 2 * (1 - xh) + lax.rem(xl + pair, 2)
        keys = jnp.concatenate([qkv[b, first, 1], qkv[b, second, 1]], axis=0)
        values = jnp.concatenate([qkv[b, first, 2], qkv[b, second, 2]], axis=0)
        return keys, values

    def mates(i, j):
        return lambda: kv_ring.landed(i, j, kv_mate)

    def out_along():
        o_ring.forward(0, True)
        send_sideways(1)
        send_sideways(2)

    def out_opposite():
        o_ring.opposite(0, True)
        send_sideways(3)

    def step(t, carry):
        def at(n, work):
            @pl.when(t == n)
            def _():
                work()

        at(1, out_along)
        at(2, lambda: send_over(0))
        at(5, out_opposite)
        at(8, lambda: send_over(1))
        at(9, lambda: send_over(2))
        at(11, lambda: send_over(3))
        at(2, lambda: kv_ring.forward(0, True))
        at(2, mates(0, 2))
        at(2, mates(1, 2))
        at(3, mates(2, 2))
        at(3, mates(3, 2))
        at(4, lambda: kv_ring.forward(1, True))
        at(6, mates(0, 4))
        at(6, mates(1, 4))
        at(6, lambda: kv_ring.forward(2, True))
        at(7, mates(0, 6))
        at(7, mates(1, 6))
        at(8, lambda: kv_ring.forward(3, True))
        at(9, lambda: kv_ring.opposite(0, True))
        at(10, mates(2, 4))
        at(10, mates(3, 4))
        at(10, lambda: kv_ring.opposite(1, True))
        at(11, mates(2, 6))
        at(11, mates(3, 6))
        at(11, lambda: kv_ring.opposite(2, True))
        own = t < 4
        place = jnp.where(own, 0, jnp.where(lax.rem(t, 2) == 0, 3, 1))
        other = jnp.where(own, lax.div(t, 2), lax.div(lax.rem(t, 4), 2))
        pair = jnp.where(own, lax.rem(t, 2), lax.div(t - 4, 4))
        keys, values = chunk_pair(place, other, pair)
        for tile in range(2):
            attend(False, keys, values, tile)
        return carry

    lax.fori_loop(0, 12, step, 0)

    def last_step(pair, tile):
        if tile == 0:

            @pl.when(pair == 0)
            def _():
                mates(0, 7)()
                mates(1, 7)()
                kv_ring.opposite(3, True)

            @pl.when(pair == 1)
            def _():
                mates(2, 7)()
                mates(3, 7)()

        for other in range(2):
            keys, values = chunk_pair(2, other, pair)
            attend(False, keys, values, tile)

    head = 2 * sp + xh

    def attended_copy(n, landing=False):
        a, b, dy = plane[n]
        at_head = head
        if landing:
            from_sp = 2 * lax.rem(y + 4 - dy, 4) + lax.rem(xl + b, 2)
            at_head = 2 * from_sp + lax.rem(xh + a, 2)
        slot = att.at[:, pl.ds(pl.multiple_of(at_head * HD, HD), HD)]
        made = slot if landing else att_out.at[((1, 0), (0, 1), (1, 1), (0, 0)).index((a, b)), lax.rem(y + dy, 4)]
        return pltpu.make_async_remote_copy(
            src_ref=made,
            dst_ref=slot,
            send_sem=at_send.at[n],
            recv_sem=at_recv.at[n],
            device_id=on_plane(a, b, dy),
            device_id_type=MESH,
        )

    for tile in range(2):
        lax.fori_loop(0, 2, lambda pair, carry: last_step(pair, tile) or carry, 0)
        for r in (2 * tile, 2 * tile + 1):
            here = pl.ds(r * keys_here, keys_here)
            total = jnp.sum(totals[here], axis=-1, keepdims=True)
            att_out[r] = (acc[here] / total).astype(BF16).reshape(4, rows, HD)
            for n in range(4 * r, min(4 * r + 4, len(plane))):
                attended_copy(n).start()
    att[:, pl.ds(pl.multiple_of(head * HD, HD), HD)] = att_out[3, y]

    for j in (4, 6, 7):
        o_ring.landed(0, j, out_mate)
    for n in range(4):
        over_copy(n, True).wait_recv()
    for n in range(len(plane)):
        attended_copy(n, True).wait_recv()

    def project(n, carry):
        columns = pl.ds(pl.multiple_of(n * 512, 512), 512)
        proj = jnp.dot(att[...], w_out[:, columns], preferred_element_type=F32)
        out_ref[:, columns] = (x_ref[:, columns].astype(F32) + gate_ref[:, columns] * proj).astype(BF16)
        return carry

    lax.fori_loop(0, width // 512, project, 0)
    final = layer_norm(out_ref[...].astype(F32)).astype(BF16)
    latent = lax.dot_general(final, w_final_ref[...], (((1,), (1,)), ((), ())), preferred_element_type=F32)
    latent = latent.astype(BF16)

    patch = latent.shape[1] // 2
    row, col = (lax.broadcasted_iota(jnp.int32, (rows, rows), d) for d in (0, 1))
    feature, lane = (lax.broadcasted_iota(jnp.int32, (2 * patch, HD), d) for d in (0, 1))
    same = lax.div(row, breadth) == lax.div(col, breadth)
    views = [jnp.zeros((rows, HD), F32)] * 2
    for d in range(3):
        shift = ((col == row + (d - 1)) & same).astype(F32).astype(BF16)
        moved = jnp.dot(shift, latent, preferred_element_type=F32).astype(BF16)
        for p in range(2):
            spread = (feature - p * patch == lane - d * patch) & (lane >= d * patch) & (lane < (d + 1) * patch)
            views[p] += jnp.dot(moved, spread.astype(F32).astype(BF16), preferred_element_type=F32)
    for p in range(2):
        for f in range(2):
            lat[f, pl.ds(p * breadth, breadth)] = views[p][f * breadth : (f + 1) * breadth].astype(BF16)

    def halo_copy(n):
        dg, ds = ways[n]
        return pltpu.make_async_remote_copy(
            src_ref=lat,
            dst_ref=window.at[pl.ds(4 - 2 * dg, 2), pl.ds(2 * breadth * (1 - ds), 2 * breadth)],
            send_sem=halo_send.at[n],
            recv_sem=halo_recv.at[n],
            device_id=(grp + dg, sp + ds),
            device_id_type=MESH,
        )

    for n, (dg, ds) in enumerate(ways):

        @pl.when(inside(dg, ds))
        def _():
            halo_copy(n).start()

    window[pl.ds(4, 2), pl.ds(2 * breadth, 2 * breadth)] = lat[...]

    first_frame = 2 * grp
    starts = []
    for f in range(4):
        clip = clip_ref[jnp.maximum(first_frame - 2 + f, 0)]
        start = 0
        for j in range(clip_ref.shape[0]):
            start = start + jnp.where(clip_ref[j] < clip, 1, 0)
        starts.append(start)

    for n, (dg, ds) in enumerate(ways):

        @pl.when(inside(-dg, -ds))
        def _():
            halo_copy(n).wait_recv()

    def frame_at(f, kt, lowest, size):
        index = jnp.maximum(first_frame - 2 + f - kt, starts[f]) - (first_frame - lowest)
        return jnp.clip(index, 0, size - 1)

    tile = lax.broadcasted_iota(jnp.int32, (4 * breadth, 1), 0)
    outside = ((tile < breadth) & (sp == 0)) | ((tile >= 3 * breadth) & (sp == tiles - 1))
    row, col = (lax.broadcasted_iota(jnp.int32, (4 * breadth, 4 * breadth), d) for d in (0, 1))
    same = lax.div(row, breadth) == lax.div(col, breadth)
    left = ((col == row - 1) & same).astype(F32).astype(BF16)
    right = ((col == row + 1) & same).astype(F32).astype(BF16)
    for f in range(4):
        seen = []
        for kt in range(3):
            index = frame_at(f, kt, 4, 6)
            seen += [window[index, pl.ds(kr * breadth, 4 * breadth)] for kr in range(3)]
        total = jnp.dot(jnp.concatenate(seen, axis=1), w_taps[...], preferred_element_type=F32)
        if f >= 2:
            direct[f - 2] = total[breadth : 3 * breadth]
        act = jnp.where(outside, 0.0, total / (1.0 + jnp.exp(-total))).astype(BF16)
        even, odd = act[:, :cv], act[:, cv:]
        planes[0, f] = jnp.dot(left, odd, preferred_element_type=F32).astype(BF16)
        planes[1, f] = even
        planes[2, f] = odd
        planes[3, f] = jnp.dot(right, even, preferred_element_type=F32).astype(BF16)

    w_mid_in.wait()
    mixed = jnp.zeros((8 * breadth, cv), F32)
    for kt in range(3):
        index = [frame_at(2 + f, kt, 2, 4) for f in range(2)]
        for kr in range(3):
            here = pl.ds(kr * breadth, 2 * breadth)
            seen = [
                jnp.concatenate([planes[q + kc, index[f], here] for kc in range(3)], axis=1)
                for f in range(2)
                for q in range(2)
            ]
            taps = weights[0, kt, pl.ds(3 * cv * kr, 3 * cv)]
            mixed = mixed + jnp.dot(jnp.concatenate(seen, axis=0), taps, preferred_element_type=F32)

    row, col = (lax.broadcasted_iota(jnp.int32, (2 * breadth, 2 * breadth), d) for d in (0, 1))
    woven = (col == lax.div(row, 2) + breadth * lax.rem(row, 2)).astype(F32).astype(BF16)
    for f in range(2):
        for r in range(2):
            pair = []
            for q in range(2):
                start = (2 * f + q) * 2 * breadth + r * breadth
                added = mixed[start : start + breadth] + direct[f, r * breadth : (r + 1) * breadth, q * cv : (q + 1) * cv]
                pair.append(added.astype(BF16))
            dec_ref[f, r] = jnp.dot(woven, jnp.concatenate(pair, axis=0), preferred_element_type=F32).astype(BF16)

    for i in range(3):
        for a in range(2):
            weight_hop(i, a).wait_send()
    for n in range(6):
        token_copy(n).wait_send()
    o_ring.finish(0, (0, 1, 3, 4, 5, 6, 7))
    for j in range(4):
        relay_copy(j).wait_send()
        near_copy(j).wait_send()
        over_copy(j).wait_send()
        for a in range(2):
            side_copy(j, a).wait_send()
            for part in range(3):
                far_copy(a, j, part).wait_send()
        kv_ring.finish(j, range(8))
    for n in range(len(plane)):
        attended_copy(n).wait_send()
    for n, (dg, ds) in enumerate(ways):

        @pl.when(inside(dg, ds))
        def _():
            halo_copy(n).wait_send()


def per_device(
    image_tokens,
    text_tokens,
    mod_shift,
    mod_scale,
    mod_gate,
    w_qkv,
    w_text_kv,
    q_gain,
    k_gain,
    text_gain,
    w_out,
    w_final,
    w_conv_in,
    w_conv_mid,
    clip_ids,
):
    slab, patch_rows, breadth, width = image_tokens.shape
    rows = slab * patch_rows * breadth
    inner_here = w_qkv.shape[2]
    inner = w_out.shape[0] * lax.axis_size("sp")
    cv = w_conv_in.shape[-1]
    head_here = lax.rem(lax.div(lax.axis_index("grp"), 2), 2)
    text_count = text_tokens.shape[0]
    w_text = lax.dynamic_slice_in_dim(w_text_kv, head_here * HD, HD, axis=2).reshape(width, 2 * HD)

    vmem = pl.BlockSpec(memory_space=pltpu.VMEM)
    anywhere = pl.BlockSpec(memory_space=pl.ANY)
    dma = pltpu.SemaphoreType.DMA
    block_flat, decoded = pl.pallas_call(
        whole_kernel,
        out_shape=(
            jax.ShapeDtypeStruct((rows, width), BF16),
            jax.ShapeDtypeStruct((slab, 2 * patch_rows, 2 * breadth, cv), BF16),
        ),
        in_specs=[vmem] * 4
        + [anywhere] * 3
        + [vmem] * 3
        + [anywhere, vmem, vmem, anywhere, pl.BlockSpec(memory_space=pltpu.SMEM)],
        out_specs=(vmem, vmem),
        scratch_shapes=[
            pltpu.VMEM((4, rows, width), BF16),
            pltpu.VMEM((2, 3, width, inner_here), BF16),
            pltpu.VMEM((8, 4, 3, 4 * rows, HD), BF16),
            pltpu.VMEM((2, 4, 2, 3, rows, HD), BF16),
            pltpu.VMEM((4, 3, rows, HD), BF16),
            pltpu.VMEM((16 * rows, HD), F32),
            pltpu.VMEM((16 * rows, HD), F32),
            pltpu.VMEM((inner, width), BF16),
            pltpu.VMEM((4, 4, rows, HD), BF16),
            pltpu.VMEM((rows, inner), BF16),
            pltpu.VMEM((text_count, width), BF16),
            pltpu.VMEM((width, 2 * HD), BF16),
            pltpu.VMEM((2, text_count, HD), BF16),
            pltpu.VMEM((2, 2 * breadth, HD), BF16),
            pltpu.VMEM((6, 6 * breadth, HD), BF16),
            pltpu.VMEM((9 * HD, 2 * cv), BF16),
            pltpu.VMEM((4, 4, 4 * breadth, cv), BF16),
            pltpu.VMEM((2, 2 * breadth, 2 * cv), F32),
            dma((5,)),
            dma((4,)),
            dma((3, 2)),
            dma((3, 2)),
            dma((3, 8)),
            dma((3, 8)),
            dma((6,)),
            dma((6,)),
            dma((1, 8)),
            dma((1, 8)),
            dma((4, 2)),
            dma((4, 2)),
            dma((4,)),
            dma((4,)),
            dma((2, 4, 3)),
            dma((2, 4, 3)),
            dma((4,)),
            dma((4,)),
            dma((4,)),
            dma((4,)),
            dma((4, 8)),
            dma((4, 8)),
            dma((15,)),
            dma((15,)),
            dma((8,)),
            dma((8,)),
        ],
        compiler_params=pltpu.CompilerParams(
            collective_id=0, has_side_effects=True, vmem_limit_bytes=60 * 1024 * 1024
        ),
    )(
        image_tokens.reshape(rows, width),
        mod_shift.reshape(1, width),
        mod_scale.reshape(1, width),
        mod_gate.reshape(1, width),
        jnp.transpose(w_qkv, (1, 0, 2)),
        text_tokens,
        w_text,
        q_gain.reshape(1, HD),
        k_gain.reshape(1, HD),
        text_gain.reshape(1, HD),
        w_out,
        jnp.transpose(w_final),
        w_conv_in,
        w_conv_mid.reshape(3, 9 * cv, cv),
        clip_ids,
    )
    return (block_flat.reshape(slab, patch_rows, breadth, width), decoded)


def solution(mesh):
    return jax.shard_map(
        per_device,
        mesh=mesh,
        in_specs=(
            P("grp", "sp", None, None),
            P(),
            P(),
            P(),
            P(),
            P(None, None, "sp"),
            P(None, None, "sp"),
            P(),
            P(),
            P(),
            P("sp", None),
            P(),
            P(),
            P(),
            P(),
        ),
        out_specs=(P("grp", "sp", None, None), P("grp", "sp", None, None)),
        check_vma=False,
    )
```

time: 149 us -> 130 us (0.87)
  Pallas kernels: 136 us -> 122 us
  other arithmetic: 4.67 us -> 0 us
    pallas_call x2 -> x1, Pallas kernels: 136 us -> 122 us  [per_device(): pl.pallas_call(whole_kernel, out_shape=(jax.ShapeDtypeStruct((rows, width...]
    reduce_sum x3 -> x0, other arithmetic: 3.92 us -> none  [the longest x1 1.96 us: layer_norm(): spread = jnp.mean(centered * centered, axis=-1, keepdims=True)]
    unnamed x18 -> x7, local copies, waits for them, and re-layouts: 4.45 us -> 6.06 us
where the time goes in v2:
time: 130 us
  Pallas kernels  122 us (94%)
  local copies, waits for them, and re-layouts  7.18 us (6%)
    pallas_call x1, Pallas kernels, per_device(): pl.pallas_call(whole_kernel, out_shape=(jax.ShapeDtypeStruct((rows, width...  122 us
    unnamed x7, local copies, waits for them, and re-layouts  6.06 us

profile of v2, /device:TPU:41, one launch (start us, length us, event | category | flops | bytes accessed | tf_op | source)
XLA Modules:
  0.0 129.5 jit_solution(12447953290968436505)
XLA Ops:
  0.6 0.0 copy-start
  0.7 1.9 %copy-done = bf16[3072,2,256]{2,1,0:T(2,128)(2,1)S(1)} copy-done((bf16[3072,2,256]{2,1,0:T(2,128)(2,1)S(1)}, bf16[3072,2,256]{2,1,0:T(2,128)(2,1)}, u32[]{:S(2)}) %copy-start) | copy-done | bytes 3145752
  2.5 1.1 constant_dynamic-slice_fusion
  3.7 1.4 %copy.20 = bf16[384,8,2,128]{3,1,2,0:T(8,128)(2,1)} copy(bf16[384,8,2,128]{3,2,1,0:T(2,128)(2,1)S(1)} %bitcast.18) | data formatting | bytes 3145728
  5.0 121.7 %shard_map.158 = (bf16[128,3072]{1,0:T(8,128)(2,1)}, bf16[2,2,128,256]{3,2,1,0:T(8,128)(2,1)}) custom-call(bf16[128,3072]{1,0:T(8,128)(2,1)} %bitcast.21, f32[1,3072]{1,0:T(1,128)} %bitcast.24, f32[1,3072]{1,0:T(1,128)} %bitcast.25, f32[1,3072]{1,0:T(1,128)} %bitcast.26, bf16[3,3072,256]{2,1,0:T(8,128)(2,1)} %bitcast.19, bf16[256,3072]{1,0:T(8,128)(2,1)} %text_ref.1, ...), custom_call_target="tpu_custom_call" | custom-call | tf_op jit(solution)/shard_map/pallas_call | solution.py:807
  126.7 0.0 copy-start.1
  126.7 2.1 %copy.23 = bf16[2,1,64,3072]{3,2,1,0:T(8,128)(2,1)} copy(bf16[2,1,64,3072]{3,2,1,0:T(8,128)(2,1)} %bitcast.22) | data formatting | bytes 1572864
  128.8 0.0 copy-done.1
  128.8 0.7 copy.24
Async XLA Ops:
  0.6 1.9 %copy-start = (bf16[3072,2,256]{2,1,0:T(2,128)(2,1)S(1)}, bf16[3072,2,256]{2,1,0:T(2,128)(2,1)}, u32[]{:S(2)}) copy-start(bf16[3072,2,256]{2,1,0:T(2,128)(2,1)} %param.21) | copy-start | bytes 9437188
  126.7 2.1 %copy-start.1 = (bf16[2,2,128,256]{3,2,1,0:T(8,128)(2,1)S(1)}, bf16[2,2,128,256]{3,2,1,0:T(8,128)(2,1)}, u32[]{:S(2)}) copy-start(bf16[2,2,128,256]{3,2,1,0:T(8,128)(2,1)} %get-tuple-element.11) | copy-start | bytes 786436

commit v3 on v2

--- a/solution.py
+++ b/solution.py
@@ -1,3 +1,4 @@
+import functools
 import math
 
 import jax
@@ -113,13 +114,14 @@
     weights,
     qkv,
     stage,
-    relay,
     acc,
     totals,
     w_out,
     att_out,
     att,
+    sums,
     text,
+    w_text_raw,
     w_text,
     text_kv,
     lat,
@@ -131,8 +133,10 @@
     copy_sem,
     wx_send,
     wx_recv,
-    w_send,
-    w_recv,
+    wz_send,
+    wz_recv,
+    wo_send,
+    wo_recv,
     t_send,
     t_recv,
     o_send,
@@ -143,8 +147,6 @@
     over_recv,
     far_send,
     far_recv,
-    relay_send,
-    relay_recv,
     near_send,
     near_recv,
     kv_send,
@@ -159,7 +161,6 @@
     y, xl = lax.div(sp, 2), lax.rem(sp, 2)
     x = 2 * xh + xl
     rows, width = x_ref.shape
-    piece_rows = width // 8
     keys_here = 4 * rows
     out_half = width // 2
 
@@ -175,7 +176,7 @@
     own_weights.start()
     text_in = pltpu.make_async_copy(text_ref, text, local_sem.at[1])
     text_in.start()
-    w_text_in = pltpu.make_async_copy(w_text_ref, w_text, local_sem.at[2])
+    w_text_in = pltpu.make_async_copy(w_text_ref, w_text_raw, local_sem.at[2])
     w_text_in.start()
     out_rows = pl.ds(pl.multiple_of(256 * sp, 256), 256)
     own_out = pltpu.make_async_copy(w_out_ref, w_out.at[out_rows], local_sem.at[3])
@@ -228,26 +229,20 @@
 
     pl.semaphore_wait(barrier, expected)
 
-    def weight_rows(place, c):
-        return pl.ds(pl.multiple_of(piece_rows * (2 * place + c), 128), piece_rows)
-
-    def weight_piece(i, place):
-        return weights.at[1 - xl, (1, 2, 0)[i], weight_rows(place, core)]
-
-    def weight_half(i, place, h):
-        start = piece_rows * (2 * place + core) + h * (piece_rows // 2)
-        return weights.at[1 - xl, (1, 2, 0)[i], pl.ds(pl.multiple_of(start, 64), piece_rows // 2)]
-
-    def weight_mate(i, place):
-        return weights.at[1 - xl, (1, 2, 0)[i], weight_rows(place, 1 - core)]
+    eighth = width // 8
+    every = (1, 2, 0)
+
+    def weight_slot(i, half, c, first, count):
+        start = eighth * (4 * half + 2 * c + first)
+        return (every[i], pl.ds(pl.multiple_of(start, eighth), eighth * count))
+
+    parity = lax.rem(z, 2)
 
     def weight_hop(i, a, landing=False):
-        part = (1, 2, 0)[i]
-        start = piece_rows * (2 * z + core) + a * (piece_rows // 2)
-        here = pl.ds(pl.multiple_of(start, 64), piece_rows // 2)
-        slot = weights.at[1 - xl if landing else xl, part, here]
-        return pltpu.make_async_remote_copy(
-            src_ref=slot if landing else w_qkv_ref.at[part, here],
+        here = weight_slot(i, parity, core, a, 1)
+        slot = weights.at[(1 - xl if landing else xl,) + here]
+        return pltpu.make_async_remote_copy(
+            src_ref=slot if landing else w_qkv_ref.at[here],
             dst_ref=slot,
             send_sem=wx_send.at[i, a],
             recv_sem=wx_recv.at[i, a],
@@ -255,11 +250,47 @@
             device_id_type=MESH,
         )
 
-    w_ring = Ring(z, device(dz=3), device(dz=1), device(dcore=1), weight_piece, weight_half, w_send, w_recv)
-
-    def weight_landed(i):
+    def weight_along(i, a, landing=False):
+        slot = weights.at[(1 - xl,) + weight_slot(i, 1 - parity if landing else parity, core, a, 1)]
+        return pltpu.make_async_remote_copy(
+            src_ref=slot,
+            dst_ref=slot,
+            send_sem=wz_send.at[i, a],
+            recv_sem=wz_recv.at[i, a],
+            device_id=device(dz=(3, 1)[a]),
+            device_id_type=MESH,
+        )
+
+    def weight_over(i, n, landing=False):
+        half = parity if n == 0 else 1 - parity
+        slot = weights.at[(1 - xl,) + weight_slot(i, half, 1 - core if landing else core, 0, 2)]
+        return pltpu.make_async_remote_copy(
+            src_ref=slot,
+            dst_ref=slot,
+            send_sem=wo_send.at[i, n],
+            recv_sem=wo_recv.at[i, n],
+            device_id=device(dcore=1),
+            device_id_type=MESH,
+        )
+
+    def weight_start(i):
+        for a in range(2):
+            weight_hop(i, a).start()
+
+    def weight_pass(i):
         for a in range(2):
             weight_hop(i, a, True).wait_recv()
+            weight_along(i, a).start()
+        weight_over(i, 0).start()
+
+    def weight_rest(i):
+        for a in range(2):
+            weight_along(i, a, True).wait_recv()
+        weight_over(i, 1).start()
+
+    def weight_ready(i):
+        for n in range(2):
+            weight_over(i, n, True).wait_recv()
 
     t_before, t_after, t_far = lax.rem(y + 3, 4), lax.rem(y + 1, 4), lax.rem(y + 2, 4)
 
@@ -276,16 +307,13 @@
             device_id_type=MESH,
         )
 
-    for i in range(3):
-        for a in range(2):
-            weight_hop(i, a).start()
+    weight_start(0)
     for h in range(2):
         here = pl.ds(h * (rows // 2), rows // 2)
         normed = layer_norm(x_ref[here].astype(F32)) * (1.0 + scale_ref[...]) + shift_ref[...]
         tokens[y, here] = normed.astype(BF16)
         token_copy(h).start()
-    token_copy(2).start()
-    token_copy(3).start()
+    weight_start(1)
 
     places = [y, t_before, t_after, t_far]
 
@@ -364,31 +392,16 @@
             device_id_type=MESH,
         )
 
-    def relay_copy(j, landing=False):
-        return pltpu.make_async_remote_copy(
-            src_ref=relay.at[j] if landing else stage.at[0, j, 1 - xh],
-            dst_ref=relay.at[j],
-            send_sem=relay_send.at[j],
-            recv_sem=relay_recv.at[j],
-            device_id=flip(j % 2, 1),
-            device_id_type=MESH,
-        )
-
     def near_copy(j, landing=False):
-        source = 2 * (1 - xh) + xl if landing else 2 * lax.rem(xh + j % 2, 2) + 1 - xl
-        slot = qkv.at[block, source, :, token_rows(j)]
-        return pltpu.make_async_remote_copy(
-            src_ref=slot if landing else relay.at[j],
+        slot = qkv.at[block, 2 * (1 - xh) + xl if landing else x, :, token_rows(j)]
+        return pltpu.make_async_remote_copy(
+            src_ref=slot if landing else stage.at[0, j, 1 - xh],
             dst_ref=slot,
             send_sem=near_send.at[j],
             recv_sem=near_recv.at[j],
-            device_id=flip(1 - j % 2, 1),
-            device_id_type=MESH,
-        )
-
-    def hand_on(j):
-        relay_copy(j, True).wait_recv()
-        near_copy(j).start()
+            device_id=flip(1, 0),
+            device_id_type=MESH,
+        )
 
     def heads(b, js, parts):
         seen = jnp.concatenate([tokens[places[j]] for j in js], axis=0)
@@ -404,39 +417,62 @@
                         far_copy(a, j, part).start()
         if b == 0:
             for j in js:
-                relay_copy(j).start()
+                near_copy(j).start()
                 own_copy(j).start()
 
-    every = (1, 2, 0)
-
     def far_heads(i, js):
-        for j in (2, 4, 6, 7):
-            w_ring.landed(i, j, weight_mate)
+        weight_ready(i)
         heads(1, js, every[i : i + 1])
 
-    for i in range(3):
-        weight_landed(i)
-        w_ring.start(i, True)
+    weight_pass(0)
+    weight_start(2)
     own_weights.wait()
     heads(0, [0], every)
-    w_ring.forward(0, True)
+    token_copy(2).start()
+    token_copy(3).start()
     own_out.wait()
     send_sideways(0)
-    hand_on(0)
+
+    w_text_in.wait()
+    row, col = (lax.broadcasted_iota(jnp.int32, (2 * HD, 4 * HD), d) for d in (0, 1))
+    chosen = (col == 4 * lax.rem(row, HD) + 2 * xh + lax.div(row, HD)).astype(F32).astype(BF16)
+
+    def choose(n, carry):
+        raw = w_text_raw[pl.ds(pl.multiple_of(n * 4 * HD, 4 * HD), 4 * HD)]
+        both = jnp.dot(chosen, raw, preferred_element_type=F32).astype(BF16)
+        here = pl.ds(pl.multiple_of(n * HD, HD), HD)
+        w_text[here, 0:HD] = both[:HD]
+        w_text[here, HD:] = both[HD:]
+        return carry
+
+    lax.fori_loop(0, width // HD // 3, choose, 0)
+    weight_pass(1)
+    lax.fori_loop(width // HD // 3, width // HD, choose, 0)
+    token_copy(0, True).wait_recv()
+    token_copy(4).start()
+    token_copy(1, True).wait_recv()
+    token_copy(5).start()
+    weight_rest(0)
+    weight_pass(2)
+    token_copy(2, True).wait_recv()
+    token_copy(3, True).wait_recv()
+    heads(0, [1, 2], every)
+    weight_rest(1)
+    far_heads(0, [0, 1, 2])
+    weight_rest(2)
+    far_heads(1, [0, 1, 2])
+    far_heads(2, [0, 1, 2])
+    token_copy(4, True).wait_recv()
+    token_copy(5, True).wait_recv()
+    heads(0, [3], every)
+    heads(1, [3], every)
+    o_ring.start(0, False)
 
     text_in.wait()
-    w_text_in.wait()
     text_normed = layer_norm(text[...].astype(F32)).astype(BF16)
     text_made = jnp.dot(text_normed, w_text[...], preferred_element_type=F32)
     text_kv[0] = rms_scale(text_made[:, :HD], text_gain_ref[...]).astype(BF16)
     text_kv[1] = text_made[:, HD:].astype(BF16)
-
-    token_copy(0, True).wait_recv()
-    token_copy(4).start()
-    token_copy(1, True).wait_recv()
-    token_copy(5).start()
-    w_ring.forward(1, True)
-    w_ring.opposite(0, True)
 
     w_taps[...] = jnp.zeros_like(w_taps)
     ch, cv = w_in_ref.shape[3], w_in_ref.shape[4]
@@ -450,24 +486,6 @@
                             first = (3 * kt + kr) * HD + (2 * d + q) * ch
                             w_taps[pl.ds(first, ch), pl.ds(cv * q_out, cv)] = w_in_ref[kt, kr, kc]
 
-    w_ring.forward(2, True)
-    token_copy(2, True).wait_recv()
-    token_copy(3, True).wait_recv()
-    heads(0, [1, 2], every)
-    w_ring.opposite(1, True)
-    far_heads(0, [0, 1, 2])
-    w_ring.opposite(2, True)
-    hand_on(1)
-    hand_on(2)
-    far_heads(1, [0, 1, 2])
-    token_copy(4, True).wait_recv()
-    token_copy(5, True).wait_recv()
-    o_ring.start(0, False)
-    heads(0, [3], every)
-    heads(1, [3], (1, 2))
-    hand_on(3)
-    far_heads(2, [0, 1, 2, 3])
-
     sources = [2 * lax.rem(xh + a, 2) + lax.rem(xl + b, 2) for b in range(2) for a in range(2)]
 
     def kv_piece_of(i, place, c):
@@ -497,7 +515,9 @@
         kv_ring.start(2 + a, True)
 
     for i in range(3):
-        w_ring.finish(i, range(8))
+        for n in range(2):
+            weight_along(i, n).wait_send()
+            weight_over(i, n).wait_send()
     w_mid = weights.at[0, :, pl.ds(0, w_mid_ref.shape[1])]
     w_mid_in = pltpu.make_async_copy(w_mid_ref, w_mid, local_sem.at[4])
     w_mid_in.start()
@@ -587,7 +607,7 @@
 
     lax.fori_loop(0, 12, step, 0)
 
-    def last_step(pair, tile):
+    def last_step(tile, pair, carry):
         if tile == 0:
 
             @pl.when(pair == 0)
@@ -604,6 +624,7 @@
         for other in range(2):
             keys, values = chunk_pair(2, other, pair)
             attend(False, keys, values, tile)
+        return carry
 
     head = 2 * sp + xh
 
@@ -625,7 +646,7 @@
         )
 
     for tile in range(2):
-        lax.fori_loop(0, 2, lambda pair, carry: last_step(pair, tile) or carry, 0)
+        lax.fori_loop(0, 2, functools.partial(last_step, tile), 0)
         for r in (2 * tile, 2 * tile + 1):
             here = pl.ds(r * keys_here, keys_here)
             total = jnp.sum(totals[here], axis=-1, keepdims=True)
@@ -638,16 +659,36 @@
         o_ring.landed(0, j, out_mate)
     for n in range(4):
         over_copy(n, True).wait_recv()
-    for n in range(len(plane)):
-        attended_copy(n, True).wait_recv()
+
+    def head_of(n):
+        a, b, dy = (plane + [(0, 0, 0)])[n]
+        return 2 * (2 * lax.rem(y + 4 - dy, 4) + lax.rem(xl + b, 2)) + lax.rem(xh + a, 2)
+
+    def head_columns(n):
+        return pl.ds(pl.multiple_of(head_of(n) * HD, HD), HD)
+
+    def projected(ns, columns):
+        seen = jnp.concatenate([att[:, head_columns(n)] for n in ns], axis=1)
+        taps = jnp.concatenate([w_out[head_columns(n), columns] for n in ns], axis=0)
+        return jnp.dot(seen, taps, preferred_element_type=F32)
 
     def project(n, carry):
         columns = pl.ds(pl.multiple_of(n * 512, 512), 512)
-        proj = jnp.dot(att[...], w_out[:, columns], preferred_element_type=F32)
+        sums[:, columns] = projected(range(8), columns)
+        return carry
+
+    def project_rest(n, carry):
+        columns = pl.ds(pl.multiple_of(n * 512, 512), 512)
+        proj = sums[:, columns] + projected(range(8, 16), columns)
         out_ref[:, columns] = (x_ref[:, columns].astype(F32) + gate_ref[:, columns] * proj).astype(BF16)
         return carry
 
+    for n in range(8):
+        attended_copy(n, True).wait_recv()
     lax.fori_loop(0, width // 512, project, 0)
+    for n in range(8, len(plane)):
+        attended_copy(n, True).wait_recv()
+    lax.fori_loop(0, width // 512, project_rest, 0)
     final = layer_norm(out_ref[...].astype(F32)).astype(BF16)
     latent = lax.dot_general(final, w_final_ref[...], (((1,), (1,)), ((), ())), preferred_element_type=F32)
     latent = latent.astype(BF16)
@@ -758,7 +799,6 @@
         token_copy(n).wait_send()
     o_ring.finish(0, (0, 1, 3, 4, 5, 6, 7))
     for j in range(4):
-        relay_copy(j).wait_send()
         near_copy(j).wait_send()
         over_copy(j).wait_send()
         for a in range(2):
@@ -773,6 +813,11 @@
         @pl.when(inside(dg, ds))
         def _():
             halo_copy(n).wait_send()
+
+
+def settle_kernel(block_ref, decoded_ref, block_out_ref, decoded_out_ref):
+    block_out_ref[...] = block_ref[...]
+    decoded_out_ref[...] = decoded_ref[...]
 
 
 def per_device(
@@ -797,9 +842,8 @@
     inner_here = w_qkv.shape[2]
     inner = w_out.shape[0] * lax.axis_size("sp")
     cv = w_conv_in.shape[-1]
-    head_here = lax.rem(lax.div(lax.axis_index("grp"), 2), 2)
     text_count = text_tokens.shape[0]
-    w_text = lax.dynamic_slice_in_dim(w_text_kv, head_here * HD, HD, axis=2).reshape(width, 2 * HD)
+    w_text = jnp.transpose(w_text_kv.reshape(width, 2, 2, HD), (0, 2, 1, 3)).reshape(4 * width, HD)
 
     vmem = pl.BlockSpec(memory_space=pltpu.VMEM)
     anywhere = pl.BlockSpec(memory_space=pl.ANY)
@@ -820,13 +864,14 @@
             pltpu.VMEM((2, 3, width, inner_here), BF16),
             pltpu.VMEM((8, 4, 3, 4 * rows, HD), BF16),
             pltpu.VMEM((2, 4, 2, 3, rows, HD), BF16),
-            pltpu.VMEM((4, 3, rows, HD), BF16),
             pltpu.VMEM((16 * rows, HD), F32),
             pltpu.VMEM((16 * rows, HD), F32),
             pltpu.VMEM((inner, width), BF16),
             pltpu.VMEM((4, 4, rows, HD), BF16),
             pltpu.VMEM((rows, inner), BF16),
+            pltpu.VMEM((rows, width), F32),
             pltpu.VMEM((text_count, width), BF16),
+            pltpu.VMEM((4 * width, HD), BF16),
             pltpu.VMEM((width, 2 * HD), BF16),
             pltpu.VMEM((2, text_count, HD), BF16),
             pltpu.VMEM((2, 2 * breadth, HD), BF16),
@@ -838,8 +883,10 @@
             dma((4,)),
             dma((3, 2)),
             dma((3, 2)),
-            dma((3, 8)),
-            dma((3, 8)),
+            dma((3, 2)),
+            dma((3, 2)),
+            dma((3, 2)),
+            dma((3, 2)),
             dma((6,)),
             dma((6,)),
             dma((1, 8)),
@@ -850,8 +897,6 @@
             dma((4,)),
             dma((2, 4, 3)),
             dma((2, 4, 3)),
-            dma((4,)),
-            dma((4,)),
             dma((4,)),
             dma((4,)),
             dma((4, 8)),
@@ -881,6 +926,12 @@
         w_conv_mid.reshape(3, 9 * cv, cv),
         clip_ids,
     )
+    block_flat, decoded = pl.pallas_call(
+        settle_kernel,
+        out_shape=tuple(jax.ShapeDtypeStruct(made.shape, made.dtype) for made in (block_flat, decoded)),
+        in_specs=[vmem] * 2,
+        out_specs=(vmem, vmem),
+    )(block_flat, decoded)
     return (block_flat.reshape(slab, patch_rows, breadth, width), decoded)
 
 

time: 130 us -> 125 us (0.962)
  local copies, waits for them, and re-layouts: 7.18 us -> 0 us
  Pallas kernels: 122 us -> 124 us
    unnamed x7 -> x0, local copies, waits for them, and re-layouts: 6.06 us -> none
    pallas_call x0 -> x1, Pallas kernels: none -> 2.2 us  [per_device(): pl.pallas_call(settle_kernel, out_shape=tuple((jax.ShapeDtypeStruct(made....]
where the time goes in v3:
time: 125 us
  Pallas kernels  124 us (99%)
    pallas_call x1, Pallas kernels, per_device(): pl.pallas_call(whole_kernel, out_shape=(jax.ShapeDtypeStruct((rows, width...  122 us

profile of v3, /device:TPU:41, one launch (start us, length us, event | category | flops | bytes accessed | tf_op | source)
XLA Modules:
  0.0 124.9 jit_solution(11797512594382961543)
XLA Ops:
  0.6 122.0 %shard_map.158 = (bf16[128,3072]{1,0:T(8,128)(2,1)}, bf16[2,2,128,256]{3,2,1,0:T(8,128)(2,1)}) custom-call(bf16[128,3072]{1,0:T(8,128)(2,1)} %bitcast.21, f32[1,3072]{1,0:T(1,128)} %bitcast.23, f32[1,3072]{1,0:T(1,128)} %bitcast.24, f32[1,3072]{1,0:T(1,128)} %bitcast.25, bf16[3,3072,256]{2,1,0:T(8,128)(2,1)} %bitcast.18, bf16[256,3072]{1,0:T(8,128)(2,1)} %text_ref.1, ...), custom_call_target="tpu_custom_call" | custom-call | tf_op jit(solution)/shard_map/pallas_call | solution.py:851
  122.7 2.2 %shard_map.159 = (bf16[128,3072]{1,0:T(8,128)(2,1)}, bf16[2,2,128,256]{3,2,1,0:T(8,128)(2,1)}) custom-call(bf16[128,3072]{1,0:T(8,128)(2,1)} %get-tuple-element.6.block_ref, bf16[2,2,128,256]{3,2,1,0:T(8,128)(2,1)} %get-tuple-element.7.decoded_ref), custom_call_target="tpu_custom_call" | custom-call | tf_op jit(solution)/shard_map/pallas_call | solution.py:929

commit v4 on v3

--- a/solution.py
+++ b/solution.py
@@ -227,6 +227,11 @@
         def _():
             window[0 : 4 - 2 * first] = jnp.zeros((4 - 2 * first, 6 * breadth, HD), BF16)
 
+    for h in range(2):
+        here = pl.ds(h * (rows // 2), rows // 2)
+        normed = layer_norm(x_ref[here].astype(F32)) * (1.0 + scale_ref[...]) + shift_ref[...]
+        tokens[y, here] = normed.astype(BF16)
+
     pl.semaphore_wait(barrier, expected)
 
     eighth = width // 8
@@ -307,12 +312,9 @@
             device_id_type=MESH,
         )
 
+    token_copy(0).start()
+    token_copy(1).start()
     weight_start(0)
-    for h in range(2):
-        here = pl.ds(h * (rows // 2), rows // 2)
-        normed = layer_norm(x_ref[here].astype(F32)) * (1.0 + scale_ref[...]) + shift_ref[...]
-        tokens[y, here] = normed.astype(BF16)
-        token_copy(h).start()
     weight_start(1)
 
     places = [y, t_before, t_after, t_far]

time: 125 us -> 125 us (level)
  no operation moved by 1% of the time
where the time goes in v4:
time: 125 us
  Pallas kernels  124 us (99%)
    pallas_call x1, Pallas kernels, per_device(): pl.pallas_call(whole_kernel, out_shape=(jax.ShapeDtypeStruct((rows, width...  122 us

profile of v4, /device:TPU:41, one launch (start us, length us, event | category | flops | bytes accessed | tf_op | source)
XLA Modules:
  0.0 124.8 jit_solution(4588431431443138746)
XLA Ops:
  0.6 122.0 %shard_map.158 = (bf16[128,3072]{1,0:T(8,128)(2,1)}, bf16[2,2,128,256]{3,2,1,0:T(8,128)(2,1)}) custom-call(bf16[128,3072]{1,0:T(8,128)(2,1)} %bitcast.21, f32[1,3072]{1,0:T(1,128)} %bitcast.23, f32[1,3072]{1,0:T(1,128)} %bitcast.24, f32[1,3072]{1,0:T(1,128)} %bitcast.25, bf16[3,3072,256]{2,1,0:T(8,128)(2,1)} %bitcast.18, bf16[256,3072]{1,0:T(8,128)(2,1)} %text_ref.1, ...), custom_call_target="tpu_custom_call" | custom-call | tf_op jit(solution)/shard_map/pallas_call | solution.py:853
  122.6 2.2 %shard_map.159 = (bf16[128,3072]{1,0:T(8,128)(2,1)}, bf16[2,2,128,256]{3,2,1,0:T(8,128)(2,1)}) custom-call(bf16[128,3072]{1,0:T(8,128)(2,1)} %get-tuple-element.6.block_ref, bf16[2,2,128,256]{3,2,1,0:T(8,128)(2,1)} %get-tuple-element.7.decoded_ref), custom_call_target="tpu_custom_call" | custom-call | tf_op jit(solution)/shard_map/pallas_call | solution.py:931
